TPU v7x, 256 devices: a whole 4x4x8 slice. The times are simulated.
256 devices in a mesh: gx: 16 (over y, x), gy: 16 (over z, core).
Axes of the slice: x: 4, y: 4, z: 8, core: 2. Of those that a mesh axis runs over, the one named last changes fastest.
Arguments:
- tree_order: int32 [256, 4096], P(('gy', 'gx')), may hold values from 0 to 4095, each once within a row
- targets: float32 [1048576, 128], P(('gy', 'gx')), may hold values from -6 to 6
- noise_var: float32 [1048576], P(('gy', 'gx')), may hold values from 0.5 to 2
- node_bases: float32 [4, 1048576, 128], P(None, ('gy', 'gx')), may hold values from -6 to 6
Outputs:
- solved: float32 [1048576, 128], P(('gy', 'gx'))
- node_weights: float32 [64, 128, 128], P('gy')
Inputs may be any that keep to these rules, and one draw needn't show every extreme that they name: Each row of tree_order is a permutation of 0 to 4095.
All inputs are finite; a program needn't handle non-finite values.
Results may differ from a plain program's by a relative error of at most 0.0001.
Values sent between devices are 32-bit elements; how exact they have to be, the bound alone decides.
No kernel may reach another device: no remote copies, remote signals or barrier semaphores. Data moves between devices by JAX's collectives and lax.ppermute only.
A program may use at most 128 MiB of HBM per device.

v0:
```python
import jax
import jax.numpy as jnp
from jax import lax
from jax.sharding import PartitionSpec as P


def chol_apply(factor, rhs):
    first = lax.linalg.triangular_solve(factor, rhs, left_side=True, lower=True)
    return lax.linalg.triangular_solve(factor, first, left_side=True, lower=True, transpose_a=True)


def on_device(tree_order, targets, noise_var, node_bases):
    order_row = tree_order[0]
    levels = node_bases.shape[0]
    rank_width = node_bases.shape[2]
    probes = targets.shape[1]
    rows_gy = lax.axis_size("gy")
    bits_gy = rows_gy.bit_length() - 1
    my_row = lax.axis_index("gy")
    all_points = order_row.shape[0] * lax.axis_size("gx") * rows_gy
    inverse_noise = (1.0 / noise_var)[:, None]
    solved_b = jnp.take(targets, order_row, axis=0) * inverse_noise
    scaled = [
        node_bases[tree_level] * (all_points / 2**tree_level) ** (-0.5)
        for tree_level in range(levels)
    ]
    solved_v = [basis_rows * inverse_noise for basis_rows in scaled]
    weights_found = [None] * levels
    for tree_level in range(levels - 1, -1, -1):
        remaining = jnp.concatenate([solved_b] + solved_v[:tree_level], axis=1)
        width_rest = remaining.shape[1]
        own_cols = solved_v[tree_level]
        columns = jnp.concatenate([remaining, own_cols], axis=1)
        gram_block = jnp.einsum(
            "pr,pc->rc", scaled[tree_level], columns, precision=lax.Precision.HIGHEST
        )
        low_bits = bits_gy - tree_level
        node_count = 2**tree_level
        node_index = my_row >> low_bits
        placed = jnp.where(
            (jnp.arange(node_count, dtype=jnp.int32) == node_index)[:, None, None],
            gram_block[None],
            0.0,
        )
        summed = lax.psum(placed, ("gx", "gy"))
        gram_block = lax.dynamic_index_in_dim(summed, node_index, 0, keepdims=False)
        gram_rest = gram_block[:, :width_rest]
        gram_own = gram_block[:, width_rest:]
        capacitance = jnp.eye(rank_width, dtype=jnp.float32) + 0.5 * (gram_own + gram_own.T)
        factor = jnp.linalg.cholesky(capacitance)
        coefficients = chol_apply(factor, gram_rest)
        remaining = remaining - jnp.dot(own_cols, coefficients, precision=lax.Precision.HIGHEST)
        solved_b = remaining[:, :probes]
        for lower in range(tree_level):
            solved_v[lower] = remaining[
                :, probes + lower * rank_width : probes + (lower + 1) * rank_width
            ]
        weights_found[tree_level] = coefficients[:, :probes]
    node_weights = jnp.stack(weights_found, axis=0)
    solved = jnp.zeros_like(solved_b).at[order_row].set(solved_b)
    return (solved, node_weights)


def solution(mesh):
    in_specs = (
        P(("gy", "gx"), None),
        P(("gy", "gx"), None),
        P(("gy", "gx")),
        P(None, ("gy", "gx"), None),
    )
    out_specs = (P(("gy", "gx"), None), P("gy", None, None))
    return jax.shard_map(
        on_device, mesh=mesh, in_specs=in_specs, out_specs=out_specs, check_vma=False
    )
```

profile of v0, /device:TPU:1, one launch (start us, length us, event | category | flops | bytes accessed | tf_op | source)
XLA Modules:
  0.0 1227.6 jit_solution(18226548815756724039)
XLA Ops:
  9.6 14.2 %gather_fusion = f32[4096,128]{1,0:T(8,128)} fusion(f32[4096,128]{1,0:T(8,128)S(1)} %copy-done, s32[4096]{0:T(1024)S(1)} %broadcast_clamp_fusion), kind=kCustom, calls=%fused_computation | custom fusion | bytes 4210688 | tf_op jit(solution)/shard_map/jit(_take)/gather | solution.py:22
  23.8 4.7 constant_dynamic-update-slice_fusion.3
  28.5 1.9 constant_dynamic-update-slice_fusion.2
  34.6 6.8 fusion.3
  43.5 265.0 %all-reduce.5.cloned.1.call-done = f32[8,128,640]{2,1,0:T(8,128)} async-done(((f32[8,128,640]{2,1,0:T(8,128)}), f32[8,128,640]{2,1,0:T(8,128)}) %all-reduce.5.cloned.1.call-update) | async-done | bytes 2621456 | tf_op jit(solution)/shard_map/psum | solution.py:45
  309.8 11.7 cholesky.74
  322.8 9.8 custom-call.22
  333.4 9.9 maximum_subtract_fusion
  343.3 8.4 fusion.4
  353.5 254.3 %all-reduce.7.cloned.1.call-done = f32[4,128,512]{2,1,0:T(8,128)} async-done(((f32[4,128,512]{2,1,0:T(8,128)}), f32[4,128,512]{2,1,0:T(8,128)}) %all-reduce.7.cloned.1.call-update) | async-done | bytes 1048592 | tf_op jit(solution)/shard_map/psum | solution.py:45
  609.0 11.7 cholesky.85
  622.0 9.8 custom-call.23
  632.6 7.8 slice_subtract_fusion
  640.4 7.9 fusion.5
  649.4 248.0 %all-reduce.9.cloned.1.call-done = f32[2,128,384]{2,1,0:T(8,128)} async-done(((f32[2,128,384]{2,1,0:T(8,128)}), f32[2,128,384]{2,1,0:T(8,128)}) %all-reduce.9.cloned.1.call-update) | async-done | bytes 393232 | tf_op jit(solution)/shard_map/psum | solution.py:45
  898.6 11.7 cholesky.96
  911.7 9.8 custom-call.24
  922.1 6.4 convolution_subtract_fusion
  930.4 6.2 fusion.13
  936.6 239.4 %all-reduce.11.cloned.1.call-done = f32[128,256]{1,0:T(8,128)} async-done(((f32[128,256]{1,0:T(8,128)}), f32[128,256]{1,0:T(8,128)}) %all-reduce.11.cloned.1.call-update) | async-done | bytes 131088 | tf_op jit(solution)/shard_map/psum | solution.py:45
  1177.9 11.7 cholesky.107
  1191.0 9.8 custom-call.25
  1202.1 5.5 convolution_subtract_fusion.1
  1207.6 12.3 %scatter_custom_fusion = f32[4096,128]{1,0:T(8,128)} fusion(s32[4096]{0:T(1024)S(1)} %bitcast.124, f32[4096,128]{1,0:T(8,128)} %convolution_subtract_fusion.1, f32[]{:T(128)} %constant.105.clone.1), kind=kCustom, calls=%fused_computation.35 | custom fusion | bytes 2097664 | tf_op jit(solution)/shard_map/scatter | solution.py:60
  (79 shorter events, 28.3 us)
Async XLA Ops:
  7.2 2.4 copy-start
  7.2 301.3 %all-reduce.5.cloned.1.call-start = ((), (), s32[]{:S(2)}) async-start(), calls=%async_computation | async-start | bytes 5242880 | tf_op jit(solution)/shard_map/psum | solution.py:45
  23.8 6.7 copy-start.2
  43.3 564.5 %all-reduce.7.cloned.1.call-start = ((), (), s32[]{:S(2)}) async-start(), calls=%async_computation.1 | async-start | bytes 2097152 | tf_op jit(solution)/shard_map/psum | solution.py:45
  343.3 8.4 copy-start.3
  353.0 544.5 %all-reduce.9.cloned.1.call-start = ((), (), s32[]{:S(2)}) async-start(), calls=%async_computation.2 | async-start | bytes 786432 | tf_op jit(solution)/shard_map/psum | solution.py:45
  640.4 7.9 copy-start.4
  649.1 526.9 %all-reduce.11.cloned.1.call-start = ((), (), s32[]{:S(2)}) async-start(), calls=%async_computation.3 | async-start | bytes 262144 | tf_op jit(solution)/shard_map/psum | solution.py:45
  928.4 1.9 copy-start.5
  1201.9 18.7 %copy-start.1 = (f32[4096,128]{1,0:T(8,128)S(1)}, f32[4096,128]{1,0:T(8,128)}, u32[]{:S(2)}) copy-start(f32[4096,128]{1,0:T(8,128)} %param.6) | copy-start | bytes 6291460
Sparse Core Ops, SparseCore 0:
  43.4 265.0 all-reduce.4
  353.1 254.6 all-reduce.6
  649.2 248.1 all-reduce.8
  936.7 239.2 all-reduce.10
where the time goes:
time: 1230 us
  waiting for transfers between devices  1010 us (82%)
  other arithmetic  110 us (9%)
  matrix products  62.2 us (5%)
  local copies, waits for them, and re-layouts  32.9 us (3%)
  between operations  14.7 us (1%)
    psum x4, waiting for transfers between devices, on_device(): summed = lax.psum(placed, ('gx', 'gy'))  1010 us
    another operation x12, other arithmetic, on_device(): factor = jnp.linalg.cholesky(capacitance)  49.6 us
    another operation x8, other arithmetic, chol_apply(): lax.linalg.triangular_solve(factor, first, left_side=True, lower=True, tr...  41.9 us
    dot_general x4, matrix products, on_device(): jnp.dot(own_cols, coefficients, precision=lax.Precision.HIGHEST)  29.5 us
    dot_general x4, matrix products, on_device(): jnp.einsum('pr,pc->rc', scaled[tree_level], columns, precision=lax.Precis...  29.3 us
  transfers between devices with their start and end apart: 4, of which 4 were waited for; matrix products, arithmetic and copies ran while one was open for 0% of the time, Pallas kernels for 0%

commit v1 on v0

v1 whole, which is shorter than its diff:
```python
import functools

import jax
import jax.numpy as jnp
from jax import lax
from jax.experimental import pallas as pl
from jax.experimental.pallas import tpu as pltpu
from jax.sharding import Mesh, PartitionSpec as P

R = 128
TILE = 1024
F32 = jnp.float32
BF16 = jnp.bfloat16
VMEM_LIMIT = 56 * 1024 * 1024


def three(a):
    a1 = a.astype(BF16)
    rest = a - a1.astype(F32)
    a2 = rest.astype(BF16)
    return a1, a2, (rest - a2.astype(F32)).astype(BF16)


def left3(a):
    a1, a2 = split(a)
    return jnp.concatenate([a1, a1, a2], axis=1)


def right3(b):
    b1, b2 = split(b)
    return jnp.concatenate([b1, b2, b1], axis=0)


def left6(a):
    a1, a2, a3 = three(a)
    return jnp.concatenate([a1, a1, a2, a1, a3, a2], axis=1)


def right6(b):
    b1, b2, b3 = three(b)
    return jnp.concatenate([b1, b2, b1, b3, b1, b2], axis=0)


def dot3(a, b):
    return dot16(left3(a), right3(b))


def dot(a, b):
    return dot16(left6(a), right6(b))


def dot16(a, b):
    return jnp.dot(a, b, preferred_element_type=F32)


def dot16_t(a, b):
    return lax.dot_general(a, b, (((0,), (0,)), ((), ())), preferred_element_type=F32)


def split(a):
    high = a.astype(BF16)
    return high, (a - high.astype(F32)).astype(BF16)


def column(rows):
    parts = [
        jnp.broadcast_to(rows[i : i + 1, :], (R, R)).T for i in range(rows.shape[0])
    ]
    return jnp.concatenate(parts, axis=0)


def block(i):
    return pl.ds(i * R, R)


def block_list(levels):
    return [(k, c) for k in range(levels - 1, -1, -1) for c in range(-1, k + 1)]


def gram_kernel(levels, scales, order, core, targets, noise, bases,
                gathered, keep, give, acc, acc_t, whole):
    step = pl.program_id(0)
    tile = bases.shape[1]
    width = levels * R

    @pl.when(step == 0)
    def _():
        acc[...] = jnp.zeros_like(acc)
        acc_t[...] = jnp.zeros_like(acc_t)

    for row in range(tile):
        gathered[pl.ds(row, 1), :] = targets[pl.ds(order[step * tile + row], 1), :]
    root = column(1.0 / jnp.sqrt(noise[pl.ds(step * (tile // R), tile // R), :]))
    pieces = [split(bases[k] * root) for k in range(levels)]
    high = jnp.concatenate([p[0] for p in pieces], axis=1)
    low = jnp.concatenate([p[1] for p in pieces], axis=1)
    right_h, right_l = split(gathered[...] * root)
    turned = high.T
    every = jnp.concatenate([high, low, right_h, right_l], axis=1)
    near = width // 2
    acc[0:near, 0:near] += dot16(turned[0:near, :], high[:, 0:near])
    acc[:, near:] += dot16(turned, every[:, near:])
    acc_t[...] += dot16(right_h.T, low)

    @pl.when(step == pl.num_programs(0) - 1)
    def _():
        blocks = block_list(levels)
        half = len(blocks) // 2
        for at, (k, c) in enumerate(blocks):
            rows = block(k)
            if c < 0:
                value = (
                    acc[rows, block(2 * levels)]
                    + acc[rows, block(2 * levels + 1)]
                    + acc_t[:, block(k)].T
                ) * scales[k]
            else:
                same = acc[rows, block(c)]
                if c < levels // 2 <= k:
                    same = acc[block(c), rows].T
                value = (
                    same
                    + acc[rows, block(levels + c)]
                    + acc[block(c), block(levels + k)].T
                ) * (scales[k] * scales[c])
            whole[block(at), :] = value
        rows = half * R

        @pl.when(core[0] == 0)
        def _():
            keep[...] = whole[0:rows, :]
            give[...] = whole[rows : 2 * rows, :]

        @pl.when(core[0] != 0)
        def _():
            give[...] = whole[0:rows, :]
            keep[...] = whole[rows : 2 * rows, :]


def grams(order, core, targets, noise, bases, scales):
    levels, points, _ = bases.shape
    half = len(block_list(levels)) // 2 * R
    width = levels * R
    grid_spec = pltpu.PrefetchScalarGridSpec(
        num_scalar_prefetch=2,
        grid=(points // TILE,),
        in_specs=[
            pl.BlockSpec((points, R), lambda i, *_: (0, 0)),
            pl.BlockSpec((points // R, R), lambda i, *_: (0, 0)),
            pl.BlockSpec((levels, TILE, R), lambda i, *_: (0, i, 0)),
        ],
        out_specs=[
            pl.BlockSpec((TILE, R), lambda i, *_: (i, 0)),
            pl.BlockSpec((half, R), lambda i, *_: (0, 0)),
            pl.BlockSpec((half, R), lambda i, *_: (0, 0)),
        ],
        scratch_shapes=[
            pltpu.VMEM((width, 2 * width + 2 * R), F32),
            pltpu.VMEM((R, width), F32),
            pltpu.VMEM((2 * half, R), F32),
        ],
    )
    return pl.pallas_call(
        functools.partial(gram_kernel, levels, scales),
        grid_spec=grid_spec,
        out_shape=[
            jax.ShapeDtypeStruct((points, R), F32),
            jax.ShapeDtypeStruct((half, R), F32),
            jax.ShapeDtypeStruct((half, R), F32),
        ],
        compiler_params=pltpu.CompilerParams(vmem_limit_bytes=VMEM_LIMIT),
        name="grams",
    )(order, core, targets, noise, bases)


def sum_kernel(copies, parts, out):
    total = parts[0]
    for i in range(1, parts.shape[0]):
        total = total + parts[i]
    for i in range(copies):
        out[i] = total


def sum_and_copy(parts):
    return pl.pallas_call(
        functools.partial(sum_kernel, parts.shape[0]),
        out_shape=jax.ShapeDtypeStruct(parts.shape, F32),
        name="sum_parts",
    )(parts)


def inverse(c, power, result):
    n = c.shape[0]
    on_diagonal = lax.broadcasted_iota(jnp.int32, (n, n), 0) == lax.broadcasted_iota(
        jnp.int32, (n, n), 1
    )
    eye = jnp.where(on_diagonal, 1.0, 0.0).astype(F32)
    diagonal = jnp.sum(c * eye, axis=0, keepdims=True)
    radius = jnp.sum(jnp.abs(c), axis=0, keepdims=True) - jnp.abs(diagonal)
    top = jnp.max(diagonal + radius)
    low = jnp.maximum(jnp.min(diagonal - radius), 1.0)
    factor = 2.0 / (low + top)
    bound = (top - low) / (low + top)
    power[...] = eye - factor * c
    result[...] = factor * (eye + power[...])

    def cond(bound):
        return bound > 1e-4

    def body(bound):
        e = dot3(power[...], power[...])
        power[...] = e
        result[...] += dot3(result[...], e)
        return bound * bound

    lax.while_loop(cond, body, bound * bound)

    def cond_r(state):
        return jnp.logical_and(state[0] > 1e-4, state[1] < 8)

    def body_r(state):
        x = result[...]
        residual = eye - dot(c, x)
        result[...] = x + dot3(x, residual)
        return jnp.max(jnp.abs(residual)), state[1] + 1

    lax.while_loop(cond_r, body_r, (jnp.float32(1.0), jnp.int32(0)))
    return result[...]


def eliminate(level, total, weights, rest, power, result):
    n = R
    own = total[block(level + 1), :]
    on_diagonal = lax.broadcasted_iota(jnp.int32, (n, n), 0) == lax.broadcasted_iota(
        jnp.int32, (n, n), 1
    )
    c = jnp.where(on_diagonal, 1.0, 0.0).astype(F32) + 0.5 * (own + own.T)
    inv = inverse(c, power, result)
    found = []
    inv = left6(inv)
    for i in range(level + 1):
        value = dot16(inv, right6(total[block(i), :]))
        weights[i] = value
        found.append(right6(value))
    at = 0
    for k in range(level - 1, -1, -1):
        left = left6(total[block(k + 1), :].T)
        for col in range(-1, k + 1):
            old = total[block(level + 2 + at), :]
            rest(at, old - dot16(left, found[col + 1]))
            at += 1


def level_kernel(level, first, core, *refs):
    if first:
        mine, other, weights, left, give, total, power, result = refs
        half = mine.shape[0]

        @pl.when(core[0] == 0)
        def _():
            total[0:half, :] = mine[...]
            total[half : 2 * half, :] = other[...]

        @pl.when(core[0] != 0)
        def _():
            total[0:half, :] = other[...]
            total[half : 2 * half, :] = mine[...]
    else:
        before, mine, other, weights, left, give, total, power, result = refs
        half = mine.shape[0]

        @pl.when(core[0] == 0)
        def _():
            total[0:half, :] = before[0:half, :] + mine[...]
            total[half : 2 * half, :] = before[half : 2 * half, :] + other[...]

        @pl.when(core[0] != 0)
        def _():
            total[0:half, :] = before[0:half, :] + other[...]
            total[half : 2 * half, :] = before[half : 2 * half, :] + mine[...]

    def put(at, value):
        left[block(at), :] = value

    eliminate(level, total, weights, put, power, result)
    size = give.shape[0]

    @pl.when(core[0] == 0)
    def _():
        give[...] = left[0:size, :]

    @pl.when(core[0] != 0)
    def _():
        give[...] = left[size : 2 * size, :]


def solve_level(level, core, incoming):
    first = len(incoming) == 2
    rows = 2 * incoming[-1].shape[0]
    after = len(block_list(level)) * R
    smem = pl.BlockSpec(memory_space=pltpu.SMEM)
    vmem = pl.BlockSpec(memory_space=pltpu.VMEM)
    return pl.pallas_call(
        functools.partial(level_kernel, level, first),
        in_specs=[smem] + [vmem] * len(incoming),
        out_specs=[vmem] * 3,
        out_shape=[
            jax.ShapeDtypeStruct((level + 1, R, R), F32),
            jax.ShapeDtypeStruct((after, R), F32),
            jax.ShapeDtypeStruct((after // 2, R), F32),
        ],
        scratch_shapes=[pltpu.VMEM((rows, R), F32)] + [pltpu.VMEM((R, R), F32)] * 2,
        compiler_params=pltpu.CompilerParams(vmem_limit_bytes=VMEM_LIMIT),
        name="level",
    )(core, *incoming)


def apply_kernel(levels, scales, order, core, before, mine, other, *refs):
    weights = refs[: levels - 1]
    noise, bases, gathered, solved, node_weights, total, coefs_h, coefs_l, held, power, result = refs[levels - 1 :]
    step = pl.program_id(0)
    tile = bases.shape[1]

    @pl.when(step == 0)
    def _():
        half = mine.shape[0]

        @pl.when(core[0] == 0)
        def _():
            total[0:half, :] = before[0:half, :] + mine[...]
            total[half : 2 * half, :] = before[half : 2 * half, :] + other[...]

        @pl.when(core[0] != 0)
        def _():
            total[0:half, :] = before[0:half, :] + other[...]
            total[half : 2 * half, :] = before[half : 2 * half, :] + mine[...]

        own = total[block(1), :]
        on_diagonal = lax.broadcasted_iota(jnp.int32, (R, R), 0) == lax.broadcasted_iota(
            jnp.int32, (R, R), 1
        )
        c = jnp.where(on_diagonal, 1.0, 0.0).astype(F32) + 0.5 * (own + own.T)
        found = [dot(inverse(c, power, result), total[block(0), :])]
        node_weights[0] = found[0]
        for k in range(1, levels):
            w = weights[k - 1]
            value = w[0]
            node_weights[k] = value
            for j in range(k):
                value = value - dot(w[j + 1], found[j])
            found.append(value)
        for k in range(levels):
            high, low = split(found[k] * scales[k])
            coefs_h[block(k), :] = high
            coefs_l[block(k), :] = low

    inverse_noise = column(1.0 / noise[pl.ds(step * (tile // R), tile // R), :])
    pieces = [split(bases[k]) for k in range(levels)]
    high = jnp.concatenate([p[0] for p in pieces], axis=1)
    low = jnp.concatenate([p[1] for p in pieces], axis=1)
    change = dot16(high, coefs_h[...]) + (dot16(high, coefs_l[...]) + dot16(low, coefs_h[...]))
    held[...] = (gathered[...] - change) * inverse_noise
    for row in range(tile):
        solved[pl.ds(order[step * tile + row], 1), :] = held[pl.ds(row, 1), :]


def apply(order, core, incoming, weights, noise, bases, gathered, scales):
    levels, points, _ = bases.shape
    whole = lambda a: pl.BlockSpec(a.shape, lambda i, *_: (0,) * a.ndim)
    grid_spec = pltpu.PrefetchScalarGridSpec(
        num_scalar_prefetch=2,
        grid=(points // TILE,),
        in_specs=[whole(a) for a in incoming]
        + [whole(a) for a in weights]
        + [
            whole(noise),
            pl.BlockSpec((levels, TILE, R), lambda i, *_: (0, i, 0)),
            pl.BlockSpec((TILE, R), lambda i, *_: (i, 0)),
        ],
        out_specs=[
            pl.BlockSpec((points, R), lambda i, *_: (0, 0)),
            pl.BlockSpec((levels, R, R), lambda i, *_: (0, 0, 0)),
        ],
        scratch_shapes=[
            pltpu.VMEM((2 * R, R), F32),
            pltpu.VMEM((levels * R, R), BF16),
            pltpu.VMEM((levels * R, R), BF16),
            pltpu.VMEM((TILE, R), F32),
            pltpu.VMEM((R, R), F32),
            pltpu.VMEM((R, R), F32),
        ],
    )
    return pl.pallas_call(
        functools.partial(apply_kernel, levels, scales),
        grid_spec=grid_spec,
        out_shape=[
            jax.ShapeDtypeStruct((points, R), F32),
            jax.ShapeDtypeStruct((levels, R, R), F32),
        ],
        compiler_params=pltpu.CompilerParams(vmem_limit_bytes=VMEM_LIMIT),
        name="apply",
    )(order, core, *incoming, *weights, noise, bases, gathered)


def on_device(tree_order, targets, noise_var, node_bases):
    levels, points, _ = node_bases.shape
    sizes = {a: lax.axis_size(a) for a in ("y", "x", "z", "c")}
    axes = ("y", "x", "z", "c")
    plane = sizes["y"] * sizes["x"]
    all_points = points * plane * sizes["z"] * sizes["c"]
    scales = [float(all_points / 2**k) ** -0.5 for k in range(levels)]
    order = tree_order[0]
    core = lax.axis_index("c").astype(jnp.int32).reshape(1)
    noise = noise_var.reshape(points // R, R)

    def swap(value, z_bit, c_bit):
        count = plane * sizes["z"] * sizes["c"]
        flip = z_bit * sizes["c"] + c_bit
        return lax.ppermute(value, axes, [(i, i ^ flip) for i in range(count)])

    gathered, keep, give = grams(order, core, targets, noise, node_bases, scales)
    mine = keep + swap(give, 0, 1)
    parts = lax.all_to_all(mine.reshape(plane, -1, R), ("y", "x"), 0, 0)
    parts = lax.all_to_all(sum_and_copy(parts), ("y", "x"), 0, 0)
    mine = parts.reshape(-1, R)
    incoming = (mine, swap(mine, 0, 1))
    weights = []
    for level in range(levels - 1, 0, -1):
        found, left, give = solve_level(level, core, incoming)
        weights.insert(0, found)
        came = swap(give, 1 << (levels - 1 - level), 0)
        incoming = (left, came, swap(came, 0, 1))
    solved, node_weights = apply(
        order, core, incoming, weights, noise, node_bases, gathered, scales
    )
    return solved, node_weights


def solution(mesh):
    fine = Mesh(mesh.devices.reshape(4, 4, 8, 2), ("y", "x", "z", "c"))
    points = ("z", "c", "y", "x")
    in_specs = (P(points, None), P(points, None), P(points), P(None, points, None))
    out_specs = (P(points, None), P(("z", "c"), None, None))
    return jax.shard_map(
        on_device, mesh=fine, in_specs=in_specs, out_specs=out_specs, check_vma=False
    )
```

time: 1230 us -> 122 us (0.10)
  waiting for transfers between devices: 1010 us -> 23.7 us
  other arithmetic: 110 us -> 1.09 us
  matrix products: 62.2 us -> 0 us
  Pallas kernels: 0 us -> 46.8 us
  local copies, waits for them, and re-layouts: 32.9 us -> 2.8 us
  blocking collectives: 0 us -> 27.3 us
  starting transfers between devices: 1.05 us -> 19.3 us
  between operations: 14.7 us -> 0.66 us
    psum x4 -> x0, waiting for transfers between devices: 1010 us -> none  [on_device(): summed = lax.psum(placed, ('gx', 'gy'))]
    another operation x21 -> x0, other arithmetic: 92.1 us -> none  [the longest x12 49.6 us: on_device(): factor = jnp.linalg.cholesky(capacitance)]
    dot_general x8 -> x0, matrix products: 58.8 us -> none  [the longest x4 29.5 us: on_device(): jnp.dot(own_cols, coefficients, precision=lax.Precision.HIGHEST)]
    pallas_call x0 -> x6, Pallas kernels: none -> 46.8 us  [the longest x3 16.9 us: solve_level(): pl.pallas_call(functools.partial(level_kernel, level, first), in_specs=[s...]
    all_to_all x0 -> x2, blocking collectives: none -> 27.3 us  [the longest x1 14.9 us: on_device(): parts = lax.all_to_all(mine.reshape(plane, -1, R), ('y', 'x'), 0, 0)]
    ppermute x0 -> x8, waiting for transfers between devices: none -> 23.7 us  [swap(): return lax.ppermute(value, axes, [(i, i ^ flip) for i in range(count)])]
    ppermute x0 -> x8, starting transfers between devices: none -> 19.3 us  [swap(): return lax.ppermute(value, axes, [(i, i ^ flip) for i in range(count)])]
    gather x1 -> x0, local copies, waits for them, and re-layouts: 14.2 us -> none  [on_device(): solved_b = jnp.take(targets, order_row, axis=0) * inverse_noise]
  transfers between devices with their start and end apart: 4 -> 8, of which waited for: 4 -> 8; matrix products, arithmetic and copies ran while one was open for 0% -> 0% of each run, Pallas kernels for 0% -> 0%
where the time goes in v1:
time: 122 us
  Pallas kernels  46.8 us (38%)
  blocking collectives  27.3 us (22%)
  waiting for transfers between devices  23.7 us (19%)
  starting transfers between devices  19.3 us (16%)
  local copies, waits for them, and re-layouts  2.8 us (2%)
    ppermute x8, waiting for transfers between devices, swap(): return lax.ppermute(value, axes, [(i, i ^ flip) for i in range(count)])  23.7 us
    ppermute x8, starting transfers between devices, swap(): return lax.ppermute(value, axes, [(i, i ^ flip) for i in range(count)])  19.3 us
    pallas_call x3, Pallas kernels, solve_level(): pl.pallas_call(functools.partial(level_kernel, level, first), in_specs=[s...  16.9 us
    all_to_all x1, blocking collectives, on_device(): parts = lax.all_to_all(mine.reshape(plane, -1, R), ('y', 'x'), 0, 0)  14.9 us
    pallas_call x1, Pallas kernels, apply(): pl.pallas_call(functools.partial(apply_kernel, levels, scales), grid_spec...  14.2 us
    pallas_call x1, Pallas kernels, grams(): pl.pallas_call(functools.partial(gram_kernel, levels, scales), grid_spec=...  13.8 us
    all_to_all x1, blocking collectives, on_device(): parts = lax.all_to_all(sum_and_copy(parts), ('y', 'x'), 0, 0)  12.4 us
    unnamed x16, local copies, waits for them, and re-layouts  2.8 us
  transfers between devices with their start and end apart: 8, of which 8 were waited for; matrix products, arithmetic and copies ran while one was open for 0% of the time, Pallas kernels for 0%

profile of v1, /device:TPU:1, one launch (start us, length us, event | category | flops | bytes accessed | tf_op | source)
XLA Modules:
  0.0 121.6 jit_solution(6422944892059775547)
XLA Ops:
  0.6 13.8 %grams.1 = (f32[4096,128]{1,0:T(8,128)}, f32[896,128]{1,0:T(8,128)}, f32[896,128]{1,0:T(8,128)}) custom-call(s32[4096]{0:T(1024)} %bitcast.8, s32[1]{0:T(128)} %bitcast.1.core, f32[4096,128]{1,0:T(8,128)} %targets.1, f32[32,128]{1,0:T(8,128)} %bitcast.10, f32[4,4096,128]{2,1,0:T(8,128)} %refs_4_.1), custom_call_target="tpu_custom_call" | custom-call | tf_op jit(solution)/shard_map/grams/pallas_call | solution.py:163
  14.4 3.2 %collective-permute-start = (f32[896,128]{1,0:T(8,128)}, f32[896,128]{1,0:T(8,128)S(1)}, u32[]{:S(2)}, u32[]{:S(2)}) collective-permute-start(f32[896,128]{1,0:T(8,128)} %get-tuple-element.15), channel_id=1, source_target_pairs={{0,1},{1,0},{2,3},{3,2},{4,5},{5,4},{6,7},{7,6},{8,9},{9,8},{10,11... | collective-permute-start | bytes 1376264 | tf_op jit(solution)/shard_map/ppermute | solution.py:419
  17.7 1.7 %collective-permute-done = f32[896,128]{1,0:T(8,128)S(1)} collective-permute-done((f32[896,128]{1,0:T(8,128)}, f32[896,128]{1,0:T(8,128)S(1)}, u32[]{:S(2)}, u32[]{:S(2)}) %collective-permute-start) | collective-permute-done | bytes 458784 | tf_op jit(solution)/shard_map/ppermute | solution.py:419
  19.3 1.1 add.3
  20.4 14.9 %all_to_all.10.parts = f32[16,56,128]{2,1,0:T(8,128)} all-to-all(f32[16,56,128]{2,1,0:T(8,128)S(1)} %bitcast.7), channel_id=1, replica_groups=mesh['y'=4,'x'=4,'z'=8,'c'=2] {'y','x'}, dimensions={0} | all-to-all | bytes 917504 | tf_op jit(solution)/shard_map/all_to_all | solution.py:423
  35.3 1.8 %sum_parts.1 = f32[16,56,128]{2,1,0:T(8,128)} custom-call(f32[16,56,128]{2,1,0:T(8,128)} %all_to_all.10.parts), custom_call_target="tpu_custom_call" | custom-call | tf_op jit(solution)/shard_map/sum_parts/pallas_call | solution.py:185
  37.1 12.4 %all_to_all.11 = f32[16,56,128]{2,1,0:T(8,128)S(1)} all-to-all(f32[16,56,128]{2,1,0:T(8,128)} %sum_parts.1), channel_id=1, replica_groups=mesh['y'=4,'x'=4,'z'=8,'c'=2] {'y','x'}, dimensions={0} | all-to-all | bytes 917504 | tf_op jit(solution)/shard_map/all_to_all | solution.py:424
  49.5 2.9 %collective-permute-start.1 = (f32[896,128]{1,0:T(8,128)S(1)}, f32[896,128]{1,0:T(8,128)S(1)}, u32[]{:S(2)}, u32[]{:S(2)}) collective-permute-start(f32[896,128]{1,0:T(8,128)S(1)} %bitcast.5), channel_id=1, source_target_pairs={{0,1},{1,0},{2,3},{3,2},{4,5},{5,4},{6,7},{7,6},{8,9},{9,8},{10,11... | collective-permute-start | bytes 1376264 | tf_op jit(solution)/shard_map/ppermute | solution.py:419
  52.4 1.4 %collective-permute-done.1.refs_1_ = f32[896,128]{1,0:T(8,128)S(1)} collective-permute-done((f32[896,128]{1,0:T(8,128)S(1)}, f32[896,128]{1,0:T(8,128)S(1)}, u32[]{:S(2)}, u32[]{:S(2)}) %collective-permute-start.1) | collective-permute-done | bytes 458784 | tf_op jit(solution)/shard_map/ppermute | solution.py:419
  54.6 5.8 %level.3 = (f32[4,128,128]{2,1,0:T(8,128)}, f32[1152,128]{1,0:T(8,128)}, f32[576,128]{1,0:T(8,128)}) custom-call(s32[1]{0:T(128)} %bitcast.1.core, f32[896,128]{1,0:T(8,128)} %bitcast.6, f32[896,128]{1,0:T(8,128)} %copy-done.1), custom_call_target="tpu_custom_call" | custom-call | tf_op jit(solution)/shard_map/level/pallas_call | solution.py:303
  60.4 2.0 %collective-permute-start.2 = (f32[576,128]{1,0:T(8,128)}, f32[576,128]{1,0:T(8,128)S(1)}, u32[]{:S(2)}, u32[]{:S(2)}) collective-permute-start(f32[576,128]{1,0:T(8,128)} %get-tuple-element.17), channel_id=1, source_target_pairs={{0,2},{1,3},{2,0},{3,1},{4,6},{5,7},{6,4},{7,5},{8,10},{9,11},{10,... | collective-permute-start | bytes 884744 | tf_op jit(solution)/shard_map/ppermute | solution.py:419
  62.3 7.3 %collective-permute-done.2.refs_1_ = f32[576,128]{1,0:T(8,128)S(1)} collective-permute-done((f32[576,128]{1,0:T(8,128)}, f32[576,128]{1,0:T(8,128)S(1)}, u32[]{:S(2)}, u32[]{:S(2)}) %collective-permute-start.2) | collective-permute-done | bytes 294944 | tf_op jit(solution)/shard_map/ppermute | solution.py:419
  70.5 1.2 collective-permute-done.3.refs_2_
  72.4 5.8 %level.4 = (f32[3,128,128]{2,1,0:T(8,128)}, f32[640,128]{1,0:T(8,128)}, f32[320,128]{1,0:T(8,128)}) custom-call(s32[1]{0:T(128)} %bitcast.1.core, f32[1152,128]{1,0:T(8,128)} %get-tuple-element.16.refs_0_, f32[576,128]{1,0:T(8,128)} %copy-done.2, f32[576,128]{1,0:T(8,128)} %copy-done.3), custom_call_target="tpu_custom_call" | custom-call | tf_op jit(solution)/shard_map/level/pallas_call | solution.py:303
  78.3 2.5 %collective-permute-start.4 = (f32[320,128]{1,0:T(8,128)}, f32[320,128]{1,0:T(8,128)S(1)}, u32[]{:S(2)}, u32[]{:S(2)}) collective-permute-start(f32[320,128]{1,0:T(8,128)} %get-tuple-element.19), channel_id=1, source_target_pairs={{0,4},{1,5},{2,6},{3,7},{4,0},{5,1},{6,2},{7,3},{8,12},{9,13},{10,... | collective-permute-start | bytes 491528 | tf_op jit(solution)/shard_map/ppermute | solution.py:419
  80.7 7.8 %collective-permute-done.4.refs_1_ = f32[320,128]{1,0:T(8,128)S(1)} collective-permute-done((f32[320,128]{1,0:T(8,128)}, f32[320,128]{1,0:T(8,128)S(1)}, u32[]{:S(2)}, u32[]{:S(2)}) %collective-permute-start.4) | collective-permute-done | bytes 163872 | tf_op jit(solution)/shard_map/ppermute | solution.py:419
  88.5 1.1 collective-permute-start.5
  89.6 1.0 collective-permute-done.5.refs_2_
  91.3 5.4 %level.5 = (f32[2,128,128]{2,1,0:T(8,128)}, f32[256,128]{1,0:T(8,128)}, f32[128,128]{1,0:T(8,128)}) custom-call(s32[1]{0:T(128)} %bitcast.1.core, f32[640,128]{1,0:T(8,128)} %get-tuple-element.18.refs_0_, f32[320,128]{1,0:T(8,128)} %copy-done.4, f32[320,128]{1,0:T(8,128)} %copy-done.5), custom_call_target="tpu_custom_call" | custom-call | tf_op jit(solution)/shard_map/level/pallas_call | solution.py:303
  96.7 6.0 %collective-permute-start.6 = (f32[128,128]{1,0:T(8,128)}, f32[128,128]{1,0:T(8,128)S(1)}, u32[]{:S(2)}, u32[]{:S(2)}) collective-permute-start(f32[128,128]{1,0:T(8,128)} %get-tuple-element.21), channel_id=1, source_target_pairs={{0,8},{1,9},{2,10},{3,11},{4,12},{5,13},{6,14},{7,15},{8,0},{9,1},... | collective-permute-start | bytes 196616 | tf_op jit(solution)/shard_map/ppermute | solution.py:419
  102.6 2.4 %collective-permute-done.6.mine = f32[128,128]{1,0:T(8,128)S(1)} collective-permute-done((f32[128,128]{1,0:T(8,128)}, f32[128,128]{1,0:T(8,128)S(1)}, u32[]{:S(2)}, u32[]{:S(2)}) %collective-permute-start.6) | collective-permute-done | bytes 65568 | tf_op jit(solution)/shard_map/ppermute | solution.py:419
  105.0 0.9 collective-permute-start.7
  105.9 0.9 collective-permute-done.7.other
  107.4 14.2 %apply.1 = (f32[4096,128]{1,0:T(8,128)}, f32[4,128,128]{2,1,0:T(8,128)}) custom-call(s32[4096]{0:T(1024)} %bitcast.9, s32[1]{0:T(128)} %bitcast.1.core, f32[256,128]{1,0:T(8,128)} %get-tuple-element.20.before, f32[128,128]{1,0:T(8,128)} %copy-done.6, f32[128,128]{1,0:T(8,128)} %copy-done.7, f32[2,128,128]{2,1,0:T(8,128)} %get-tuple-element.22.refs_0_, ...), custom_call_target="tpu_custom_call" | custom-call | tf_op jit(solution)/shard_map/apply/pallas_call | solution.py:393
  (17 shorter events, 3.7 us)
Async XLA Ops:
  14.4 4.9 %collective-permute-start = (f32[896,128]{1,0:T(8,128)}, f32[896,128]{1,0:T(8,128)S(1)}, u32[]{:S(2)}, u32[]{:S(2)}) collective-permute-start(f32[896,128]{1,0:T(8,128)} %get-tuple-element.15), channel_id=1, source_target_pairs={{0,1},{1,0},{2,3},{3,2},{4,5},{5,4},{6,7},{7,6},{8,9},{9,8},{10,11... | collective-permute-start | bytes 1376264 | tf_op jit(solution)/shard_map/ppermute | solution.py:419
  49.5 4.3 %copy-start = (f32[16,56,128]{2,1,0:T(8,128)}, f32[16,56,128]{2,1,0:T(8,128)S(1)}, u32[]{:S(2)}) copy-start(f32[16,56,128]{2,1,0:T(8,128)S(1)} %all_to_all.11) | copy-start | bytes 1376260
  49.5 4.3 %collective-permute-start.1 = (f32[896,128]{1,0:T(8,128)S(1)}, f32[896,128]{1,0:T(8,128)S(1)}, u32[]{:S(2)}, u32[]{:S(2)}) collective-permute-start(f32[896,128]{1,0:T(8,128)S(1)} %bitcast.5), channel_id=1, source_target_pairs={{0,1},{1,0},{2,3},{3,2},{4,5},{5,4},{6,7},{7,6},{8,9},{9,8},{10,11... | collective-permute-start | bytes 1376264 | tf_op jit(solution)/shard_map/ppermute | solution.py:419
  53.8 0.8 copy-start.1
  60.4 9.3 %collective-permute-start.2 = (f32[576,128]{1,0:T(8,128)}, f32[576,128]{1,0:T(8,128)S(1)}, u32[]{:S(2)}, u32[]{:S(2)}) collective-permute-start(f32[576,128]{1,0:T(8,128)} %get-tuple-element.17), channel_id=1, source_target_pairs={{0,2},{1,3},{2,0},{3,1},{4,6},{5,7},{6,4},{7,5},{8,10},{9,11},{10,... | collective-permute-start | bytes 884744 | tf_op jit(solution)/shard_map/ppermute | solution.py:419
  69.6 2.1 %copy-start.2 = (f32[576,128]{1,0:T(8,128)}, f32[576,128]{1,0:T(8,128)S(1)}, u32[]{:S(2)}) copy-start(f32[576,128]{1,0:T(8,128)S(1)} %collective-permute-done.2.refs_1_) | copy-start | bytes 884740
  69.6 2.1 %collective-permute-start.3 = (f32[576,128]{1,0:T(8,128)S(1)}, f32[576,128]{1,0:T(8,128)S(1)}, u32[]{:S(2)}, u32[]{:S(2)}) collective-permute-start(f32[576,128]{1,0:T(8,128)S(1)} %collective-permute-done.2.refs_1_), channel_id=1, source_target_pairs={{0,1},{1,0},{2,3},{3,2},{4,5},{5,4},{6,7},{7,6},{8,9},{9,8},{10,11... | collective-permute-start | bytes 884744 | tf_op jit(solution)/shard_map/ppermute | solution.py:419
  71.7 0.7 copy-start.3
  78.3 10.3 %collective-permute-start.4 = (f32[320,128]{1,0:T(8,128)}, f32[320,128]{1,0:T(8,128)S(1)}, u32[]{:S(2)}, u32[]{:S(2)}) collective-permute-start(f32[320,128]{1,0:T(8,128)} %get-tuple-element.19), channel_id=1, source_target_pairs={{0,4},{1,5},{2,6},{3,7},{4,0},{5,1},{6,2},{7,3},{8,12},{9,13},{10,... | collective-permute-start | bytes 491528 | tf_op jit(solution)/shard_map/ppermute | solution.py:419
  88.5 2.1 %copy-start.4 = (f32[320,128]{1,0:T(8,128)}, f32[320,128]{1,0:T(8,128)S(1)}, u32[]{:S(2)}) copy-start(f32[320,128]{1,0:T(8,128)S(1)} %collective-permute-done.4.refs_1_) | copy-start | bytes 491524
  88.5 2.1 %collective-permute-start.5 = (f32[320,128]{1,0:T(8,128)S(1)}, f32[320,128]{1,0:T(8,128)S(1)}, u32[]{:S(2)}, u32[]{:S(2)}) collective-permute-start(f32[320,128]{1,0:T(8,128)S(1)} %collective-permute-done.4.refs_1_), channel_id=1, source_target_pairs={{0,1},{1,0},{2,3},{3,2},{4,5},{5,4},{6,7},{7,6},{8,9},{9,8},{10,11... | collective-permute-start | bytes 491528 | tf_op jit(solution)/shard_map/ppermute | solution.py:419
  90.6 0.7 copy-start.5
  96.7 8.3 %collective-permute-start.6 = (f32[128,128]{1,0:T(8,128)}, f32[128,128]{1,0:T(8,128)S(1)}, u32[]{:S(2)}, u32[]{:S(2)}) collective-permute-start(f32[128,128]{1,0:T(8,128)} %get-tuple-element.21), channel_id=1, source_target_pairs={{0,8},{1,9},{2,10},{3,11},{4,12},{5,13},{6,14},{7,15},{8,0},{9,1},... | collective-permute-start | bytes 196616 | tf_op jit(solution)/shard_map/ppermute | solution.py:419
  105.0 1.8 %copy-start.6 = (f32[128,128]{1,0:T(8,128)}, f32[128,128]{1,0:T(8,128)S(1)}, u32[]{:S(2)}) copy-start(f32[128,128]{1,0:T(8,128)S(1)} %collective-permute-done.6.mine) | copy-start | bytes 196612
  105.0 1.8 %collective-permute-start.7 = (f32[128,128]{1,0:T(8,128)S(1)}, f32[128,128]{1,0:T(8,128)S(1)}, u32[]{:S(2)}, u32[]{:S(2)}) collective-permute-start(f32[128,128]{1,0:T(8,128)S(1)} %collective-permute-done.6.mine), channel_id=1, source_target_pairs={{0,1},{1,0},{2,3},{3,2},{4,5},{5,4},{6,7},{7,6},{8,9},{9,8},{10,11... | collective-permute-start | bytes 196616 | tf_op jit(solution)/shard_map/ppermute | solution.py:419
  106.8 0.6 copy-start.7

commit v2 on v1

v2 whole, which is shorter than its diff:
```python
import functools

import jax
import jax.numpy as jnp
from jax import lax
from jax.experimental import pallas as pl
from jax.experimental.pallas import tpu as pltpu
from jax.sharding import Mesh, PartitionSpec as P

R = 128
TILE = 1024
F32 = jnp.float32
BF16 = jnp.bfloat16
MIB = 1024 * 1024


def three(a):
    a1 = a.astype(BF16)
    rest = a - a1.astype(F32)
    a2 = rest.astype(BF16)
    return a1, a2, (rest - a2.astype(F32)).astype(BF16)


def left3(a):
    a1, a2 = split(a)
    return jnp.concatenate([a1, a1, a2], axis=1)


def right3(b):
    b1, b2 = split(b)
    return jnp.concatenate([b1, b2, b1], axis=0)


def left6(a):
    a1, a2, a3 = three(a)
    return jnp.concatenate([a1, a1, a2, a1, a3, a2], axis=1)


def right6(b):
    b1, b2, b3 = three(b)
    return jnp.concatenate([b1, b2, b1, b3, b1, b2], axis=0)


def dot3(a, b):
    return dot16(left3(a), right3(b))


def dot(a, b):
    return dot16(left6(a), right6(b))


def dot16(a, b):
    return jnp.dot(a, b, preferred_element_type=F32)


def dot16_t(a, b):
    return lax.dot_general(a, b, (((0,), (0,)), ((), ())), preferred_element_type=F32)


def split(a):
    high = a.astype(BF16)
    return high, (a - high.astype(F32)).astype(BF16)


def column(rows):
    parts = [
        jnp.broadcast_to(rows[i : i + 1, :], (R, R)).T for i in range(rows.shape[0])
    ]
    return jnp.concatenate(parts, axis=0)


def block(i):
    return pl.ds(i * R, R)


def block_list(levels):
    return [(k, c) for k in range(levels - 1, -1, -1) for c in range(-1, k + 1)]


def gram_kernel(levels, scales, order, core, targets, noise, bases,
                keep, give, acc, acc_t, whole, gathered):
    step = pl.program_id(0)
    tile = bases.shape[1]
    width = levels * R

    @pl.when(step == 0)
    def _():
        acc[...] = jnp.zeros_like(acc)
        acc_t[...] = jnp.zeros_like(acc_t)

    for row in range(tile):
        gathered[pl.ds(row, 1), :] = targets[pl.ds(order[step * tile + row], 1), :]
    root = column(1.0 / jnp.sqrt(noise[pl.ds(step * (tile // R), tile // R), :]))
    pieces = [split(bases[k] * root) for k in range(levels)]
    high = jnp.concatenate([p[0] for p in pieces], axis=1)
    low = jnp.concatenate([p[1] for p in pieces], axis=1)
    right_h, right_l = split(gathered[...] * root)
    turned = high.T
    every = jnp.concatenate([high, low, right_h, right_l], axis=1)
    near = width // 2
    acc[0:near, 0:near] += dot16(turned[0:near, :], high[:, 0:near])
    acc[:, near:] += dot16(turned, every[:, near:])
    acc_t[...] += dot16(right_h.T, low)

    @pl.when(step == pl.num_programs(0) - 1)
    def _():
        blocks = block_list(levels)
        half = len(blocks) // 2
        for at, (k, c) in enumerate(blocks):
            rows = block(k)
            if c < 0:
                value = (
                    acc[rows, block(2 * levels)]
                    + acc[rows, block(2 * levels + 1)]
                    + acc_t[:, block(k)].T
                ) * scales[k]
            else:
                same = acc[rows, block(c)]
                if c < levels // 2 <= k:
                    same = acc[block(c), rows].T
                value = (
                    same
                    + acc[rows, block(levels + c)]
                    + acc[block(c), block(levels + k)].T
                ) * (scales[k] * scales[c])
            whole[block(at), :] = value
        rows = half * R

        @pl.when(core[0] == 0)
        def _():
            keep[...] = whole[0:rows, :]
            give[...] = whole[rows : 2 * rows, :]

        @pl.when(core[0] != 0)
        def _():
            give[...] = whole[0:rows, :]
            keep[...] = whole[rows : 2 * rows, :]


def grams(order, core, targets, noise, bases, scales):
    levels, points, _ = bases.shape
    half = len(block_list(levels)) // 2 * R
    width = levels * R
    grid_spec = pltpu.PrefetchScalarGridSpec(
        num_scalar_prefetch=2,
        grid=(points // TILE,),
        in_specs=[
            pl.BlockSpec((points, R), lambda i, *_: (0, 0)),
            pl.BlockSpec((points // R, R), lambda i, *_: (0, 0)),
            pl.BlockSpec((levels, TILE, R), lambda i, *_: (0, i, 0)),
        ],
        out_specs=[
            pl.BlockSpec((half, R), lambda i, *_: (0, 0)),
            pl.BlockSpec((half, R), lambda i, *_: (0, 0)),
        ],
        scratch_shapes=[
            pltpu.VMEM((width, 2 * width + 2 * R), F32),
            pltpu.VMEM((R, width), F32),
            pltpu.VMEM((2 * half, R), F32),
            pltpu.VMEM((TILE, R), F32),
        ],
    )
    return pl.pallas_call(
        functools.partial(gram_kernel, levels, scales),
        grid_spec=grid_spec,
        out_shape=[
            jax.ShapeDtypeStruct((half, R), F32),
            jax.ShapeDtypeStruct((half, R), F32),
        ],
        compiler_params=pltpu.CompilerParams(vmem_limit_bytes=56 * MIB),
        name="grams",
    )(order, core, targets, noise, bases)


def sum_kernel(copies, parts, out):
    total = parts[0]
    for i in range(1, parts.shape[0]):
        total = total + parts[i]
    for i in range(copies):
        out[i] = total


def sum_and_copy(parts):
    return pl.pallas_call(
        functools.partial(sum_kernel, parts.shape[0]),
        out_shape=jax.ShapeDtypeStruct(parts.shape, F32),
        compiler_params=pltpu.CompilerParams(vmem_limit_bytes=8 * MIB),
        name="sum_parts",
    )(parts)


def inverse(c, power, result):
    n = c.shape[0]
    on_diagonal = lax.broadcasted_iota(jnp.int32, (n, n), 0) == lax.broadcasted_iota(
        jnp.int32, (n, n), 1
    )
    eye = jnp.where(on_diagonal, 1.0, 0.0).astype(F32)
    diagonal = jnp.sum(c * eye, axis=0, keepdims=True)
    radius = jnp.sum(jnp.abs(c), axis=0, keepdims=True) - jnp.abs(diagonal)
    top = jnp.max(diagonal + radius)
    low = jnp.maximum(jnp.min(diagonal - radius), 1.0)
    factor = 2.0 / (low + top)
    bound = (top - low) / (low + top)
    power[...] = eye - factor * c
    result[...] = factor * (eye + power[...])

    def cond(bound):
        return bound > 1e-4

    def body(bound):
        e = dot3(power[...], power[...])
        power[...] = e
        result[...] += dot3(result[...], e)
        return bound * bound

    lax.while_loop(cond, body, bound * bound)

    def cond_r(state):
        return jnp.logical_and(state[0] > 1e-4, state[1] < 8)

    def body_r(state):
        x = result[...]
        residual = eye - dot(c, x)
        result[...] = x + dot3(x, residual)
        return jnp.max(jnp.abs(residual)), state[1] + 1

    lax.while_loop(cond_r, body_r, (jnp.float32(1.0), jnp.int32(0)))
    return result[...]


def capacitance(own):
    n = own.shape[0]
    on_diagonal = lax.broadcasted_iota(jnp.int32, (n, n), 0) == lax.broadcasted_iota(
        jnp.int32, (n, n), 1
    )
    return jnp.where(on_diagonal, 1.0, 0.0).astype(F32) + 0.5 * (own + own.T)


def eliminate(level, total, weights, left, give, core, power, result):
    get = lambda i: total[block(i), :]
    inv = left6(inverse(capacitance(get(level + 1)), power, result))
    found = []
    for i in range(level + 1):
        value = dot16(inv, right6(get(i)))
        weights[i] = value
        found.append(right6(value))
    for i, (k, col) in enumerate(block_list(level)):
        if col < 0:
            turned = left6(get(k + 1).T)
        left[block(i), :] = get(level + 2 + i) - dot16(turned, found[col + 1])
    if give is None:
        return
    size = give.shape[0]

    @pl.when(core[0] == 0)
    def _():
        give[...] = left[0:size, :]

    @pl.when(core[0] != 0)
    def _():
        give[...] = left[size : 2 * size, :]


def join(core, total, mine, other, before=None):
    half = mine.shape[0]
    for first in (0, 1):

        @pl.when(core[0] == first)
        def _():
            for place, part in ((first * half, mine), ((1 - first) * half, other)):
                value = part[...]
                if before is not None:
                    value = value + before[place : place + half, :]
                total[place : place + half, :] = value


def level_kernel(level, first, core, *refs):
    refs = list(refs)
    before = None if first else refs.pop(0)
    mine, other, weights, left, *give, total, power, result = refs
    join(core, total, mine, other, before)
    eliminate(level, total, weights, left, give[0] if give else None, core, power, result)


def solve_level(level, core, incoming):
    first = len(incoming) == 2
    after = len(block_list(level))
    smem = pl.BlockSpec(memory_space=pltpu.SMEM)
    vmem = pl.BlockSpec(memory_space=pltpu.VMEM)
    rows = 2 * incoming[-1].shape[0]
    shapes = [(level + 1, R, R), (after * R, R)]
    if level > 1:
        shapes.append((after * R // 2, R))
    return pl.pallas_call(
        functools.partial(level_kernel, level, first),
        in_specs=[smem] + [vmem] * len(incoming),
        out_specs=[vmem] * len(shapes),
        out_shape=[jax.ShapeDtypeStruct(shape, F32) for shape in shapes],
        scratch_shapes=[pltpu.VMEM((rows, R), F32)] + [pltpu.VMEM((R, R), F32)] * 2,
        compiler_params=pltpu.CompilerParams(vmem_limit_bytes=12 * MIB),
        name="level",
    )(core, *incoming)


def moves(order, start, count, pairs):
    def some(at, _):
        for j in range(64):
            row = at * 64 + j
            to = pl.ds(order[start + row], 1)
            for source, target in pairs:
                target[to, :] = source[pl.ds(start + row, 1), :]
        return 0

    lax.fori_loop(0, count // 64, some, 0)


def place_kernel(levels, with_base, order, noise, bases, *refs):
    count = len(levels)
    if with_base:
        targets, refs = refs[0], refs[1:]
    outs, refs = refs[: 2 * count], refs[2 * count :]
    if with_base:
        base, refs = refs[0], refs[1:]
    held, placed, made, in_sem, out_sem, *refs = refs
    if with_base:
        root, spread, given, based = refs
    points = held.shape[1]
    tiles = points // TILE

    def load(t, k):
        rows = pl.ds(t * TILE, TILE)
        return pltpu.make_async_copy(
            bases.at[levels[k], rows, :], held.at[k, rows, :], in_sem.at[t, k]
        )

    def save(t, i):
        rows = pl.ds(t * TILE, TILE)
        if i == 2 * count:
            return pltpu.make_async_copy(based.at[rows, :], base.at[rows, :], out_sem.at[t, i])
        return pltpu.make_async_copy(made.at[i, rows, :], outs[i].at[rows, :], out_sem.at[t, i])

    for t in range(tiles):
        for k in range(count):
            load(t, k).start()
    if with_base:
        late = pltpu.make_async_copy(targets, given, in_sem.at[0, count])
        late.start()
    for t in range(tiles):
        rows = pl.ds(t * TILE, TILE)
        over = column(1.0 / noise[pl.ds(t * (TILE // R), TILE // R), :])
        for k in range(count):
            load(t, k).wait()
            held[k, rows, :] = held[k, rows, :] * over
        pairs = [(held.at[k], placed.at[k]) for k in range(count)]
        if with_base:
            root[rows, :] = over
            pairs.append((root, spread))
        moves(order, t * TILE, TILE, pairs)
    if with_base:
        late.wait()
    for t in range(tiles):
        rows = pl.ds(t * TILE, TILE)
        for k in range(count):
            made[2 * k, rows, :], made[2 * k + 1, rows, :] = split(placed[k, rows, :])
        if with_base:
            based[rows, :] = given[rows, :] * spread[rows, :]
        for i in range(2 * count + with_base):
            save(t, i).start()
    for t in range(tiles):
        for i in range(2 * count + with_base):
            save(t, i).wait()


def place(order, noise, bases, levels, targets=None):
    points = order.shape[0]
    count, tiles = len(levels), points // TILE
    with_base = targets is not None
    anywhere = pl.BlockSpec(memory_space=pl.ANY)
    one = pltpu.VMEM((points, R), F32)
    return pl.pallas_call(
        functools.partial(place_kernel, levels, with_base),
        in_specs=[
            pl.BlockSpec(memory_space=pltpu.SMEM),
            pl.BlockSpec(memory_space=pltpu.VMEM),
        ]
        + [anywhere] * (1 + with_base),
        out_specs=[anywhere] * (2 * count + with_base),
        out_shape=[jax.ShapeDtypeStruct((points, R), BF16)] * (2 * count)
        + [jax.ShapeDtypeStruct((points, R), F32)] * with_base,
        scratch_shapes=[
            pltpu.VMEM((count, points, R), F32),
            pltpu.VMEM((count, points, R), F32),
            pltpu.VMEM((2 * count, points, R), BF16),
            pltpu.SemaphoreType.DMA((tiles, count + 1)),
            pltpu.SemaphoreType.DMA((tiles, 2 * count + 1)),
        ]
        + [one] * (4 * with_base),
        compiler_params=pltpu.CompilerParams(vmem_limit_bytes=52 * MIB),
        cost_estimate=pl.CostEstimate(
            flops=points * R * 40, bytes_accessed=11 * MIB, transcendentals=0
        ),
        name="place",
    )(order, noise, bases, *([targets] if with_base else []))


def apply_kernel(levels, scales, left, came, *refs):
    weights, refs = refs[: levels - 1], refs[levels - 1 :]
    given, refs = refs[: 2 * levels + 1], refs[2 * levels + 1 :]
    solved, node_weights, highs, lows, base, out, coefs, power, result, in_sem, out_sem = refs
    points = base.shape[0]
    tiles = points // TILE

    def copies(t):
        rows = pl.ds(t * TILE, TILE)
        made = []
        for i, source in enumerate(given):
            if i == 2 * levels:
                target = base.at[rows, :]
            else:
                target = (highs, lows)[i % 2].at[rows, block(i // 2)]
            made.append(pltpu.make_async_copy(source.at[rows, :], target, in_sem.at[t, i]))
        return made

    def write(t):
        rows = pl.ds(t * TILE, TILE)
        return pltpu.make_async_copy(out.at[rows, :], solved.at[rows, :], out_sem.at[t])

    for t in range(tiles):
        for copy in copies(t):
            copy.start()
    total = left[...] + came[...]
    inv = inverse(capacitance(total[R:, :]), power, result)
    found = [dot(inv, total[:R, :])]
    node_weights[0] = found[0]
    for k in range(1, levels):
        w = weights[k - 1]
        value = w[0]
        node_weights[k] = value
        for j in range(k):
            value = value - dot(w[j + 1], found[j])
        found.append(value)
    for k in range(levels):
        h, l = split(found[k] * scales[k])
        coefs[block(k), 0:R] = h
        coefs[block(k), R : 2 * R] = l
    for t in range(tiles):
        rows = pl.ds(t * TILE, TILE)
        for copy in copies(t):
            copy.wait()
        both = dot16(highs[rows, :], coefs[...])
        small = both[:, R : 2 * R] + dot16(lows[rows, :], coefs[:, 0:R])
        out[rows, :] = base[rows, :] - (both[:, 0:R] + small)
        write(t).start()
    for t in range(tiles):
        write(t).wait()


def apply(incoming, weights, placed, base, scales):
    points = base.shape[0]
    levels = len(scales)
    tiles = points // TILE
    vmem = pl.BlockSpec(memory_space=pltpu.VMEM)
    anywhere = pl.BlockSpec(memory_space=pl.ANY)
    return pl.pallas_call(
        functools.partial(apply_kernel, levels, scales),
        in_specs=[vmem] * (len(incoming) + len(weights)) + [anywhere] * (len(placed) + 1),
        out_specs=[anywhere, vmem],
        out_shape=[
            jax.ShapeDtypeStruct((points, R), F32),
            jax.ShapeDtypeStruct((levels, R, R), F32),
        ],
        scratch_shapes=[
            pltpu.VMEM((points, levels * R), BF16),
            pltpu.VMEM((points, levels * R), BF16),
            pltpu.VMEM((points, R), F32),
            pltpu.VMEM((points, R), F32),
            pltpu.VMEM((levels * R, 2 * R), BF16),
            pltpu.VMEM((R, R), F32),
            pltpu.VMEM((R, R), F32),
            pltpu.SemaphoreType.DMA((tiles, 2 * levels + 1)),
            pltpu.SemaphoreType.DMA((tiles,)),
        ],
        compiler_params=pltpu.CompilerParams(vmem_limit_bytes=52 * MIB),
        name="apply",
    )(*incoming, *weights, *placed, base)


def on_device(tree_order, targets, noise_var, node_bases):
    levels, points, _ = node_bases.shape
    sizes = {a: lax.axis_size(a) for a in ("y", "x", "z", "c")}
    axes = ("y", "x", "z", "c")
    plane = sizes["y"] * sizes["x"]
    all_points = points * plane * sizes["z"] * sizes["c"]
    scales = [float(all_points / 2**k) ** -0.5 for k in range(levels)]
    order = tree_order[0]
    core = lax.axis_index("c").astype(jnp.int32).reshape(1)
    noise = noise_var.reshape(points // R, R)

    def swap(value, z_bit, c_bit):
        count = plane * sizes["z"] * sizes["c"]
        flip = z_bit * sizes["c"] + c_bit
        return lax.ppermute(value, axes, [(i, i ^ flip) for i in range(count)])

    keep, give = grams(order, core, targets, noise, node_bases, scales)
    mine = keep + swap(give, 0, 1)

    def beside(value, move, picked, extra=None):
        value, when = lax.optimization_barrier((value, order))
        value = move(value)
        made = place(when, noise, node_bases, picked, extra)
        value, *made = lax.optimization_barrier((value, *made))
        return value, made

    spread = lambda a: lax.all_to_all(a, ("y", "x"), 0, 0)
    half = levels // 2
    parts, (*placed, base) = beside(
        mine.reshape(plane, -1, R), spread, list(range(half)), targets
    )
    parts, more = beside(sum_and_copy(parts), spread, list(range(half, levels)))
    placed += more
    mine = parts.reshape(-1, R)
    incoming = (mine, swap(mine, 0, 1))
    weights = []
    for level in range(levels - 1, 0, -1):
        found, left, *give = solve_level(level, core, incoming)
        weights.insert(0, found)
        if give:
            came = swap(give[0], 1 << (levels - 1 - level), 0)
            incoming = (left, came, swap(came, 0, 1))
    came = swap(left, sizes["z"] - 1, 0)
    return tuple(apply((left, came), weights, placed, base, scales))


def solution(mesh):
    fine = Mesh(mesh.devices.reshape(4, 4, 8, 2), ("y", "x", "z", "c"))
    points = ("z", "c", "y", "x")
    in_specs = (P(points, None), P(points, None), P(points), P(None, points, None))
    out_specs = (P(points, None), P(("z", "c"), None, None))
    return jax.shard_map(
        on_device, mesh=fine, in_specs=in_specs, out_specs=out_specs, check_vma=False
    )
```

time: 122 us -> 113 us (0.926)
  blocking collectives: 27.3 us -> 0 us
  starting transfers between devices: 19.3 us -> 28.1 us
  Pallas kernels: 46.8 us -> 55 us
  waiting for transfers between devices: 23.7 us -> 25.9 us
  local copies, waits for them, and re-layouts: 2.8 us -> 1.06 us
    all_to_all x2 -> x0, blocking collectives: 27.3 us -> none  [the longest x1 14.9 us: on_device(): parts = lax.all_to_all(mine.reshape(plane, -1, R), ('y', 'x'), 0, 0)]
    pallas_call x1 -> x3, Pallas kernels: 14.2 us -> 29.5 us  [the longest x2 20.7 us: place(): pl.pallas_call(functools.partial(place_kernel, levels, with_base), in_spe...]
    all_to_all x0 -> x2, starting transfers between devices: none -> 11.7 us  [on_device(): spread = lambda a: lax.all_to_all(a, ('y', 'x'), 0, 0)]
    pallas_call x3, Pallas kernels: 16.9 us -> 11.2 us  [solve_level(): pl.pallas_call(functools.partial(level_kernel, level, first), in_specs=[s...]
    ppermute x8 -> x7, starting transfers between devices: 19.3 us -> 16.4 us  [swap(): return lax.ppermute(value, axes, [(i, i ^ flip) for i in range(count)])]
    ppermute x8 -> x7, waiting for transfers between devices: 23.7 us -> 25.9 us  [swap(): return lax.ppermute(value, axes, [(i, i ^ flip) for i in range(count)])]
    unnamed x16 -> x6, local copies, waits for them, and re-layouts: 2.8 us -> 1.06 us
  transfers between devices with their start and end apart: 8 -> 9, of which waited for: 8 -> 7; matrix products, arithmetic and copies ran while one was open for 0% -> 0% of each run, Pallas kernels for 0% -> 18%
where the time goes in v2:
time: 113 us
  Pallas kernels  55 us (49%)
  starting transfers between devices  28.1 us (25%)
  waiting for transfers between devices  25.9 us (23%)
  other arithmetic  1.85 us (2%)
    ppermute x7, waiting for transfers between devices, swap(): return lax.ppermute(value, axes, [(i, i ^ flip) for i in range(count)])  25.9 us
    pallas_call x2, Pallas kernels, place(): pl.pallas_call(functools.partial(place_kernel, levels, with_base), in_spe...  20.7 us
    ppermute x7, starting transfers between devices, swap(): return lax.ppermute(value, axes, [(i, i ^ flip) for i in range(count)])  16.4 us
    pallas_call x1, Pallas kernels, grams(): pl.pallas_call(functools.partial(gram_kernel, levels, scales), grid_spec=...  13.5 us
    all_to_all x2, starting transfers between devices, on_device(): spread = lambda a: lax.all_to_all(a, ('y', 'x'), 0, 0)  11.7 us
    pallas_call x3, Pallas kernels, solve_level(): pl.pallas_call(functools.partial(level_kernel, level, first), in_specs=[s...  11.2 us
    pallas_call x1, Pallas kernels, apply(): pl.pallas_call(functools.partial(apply_kernel, levels, scales), in_specs=...  8.81 us
  transfers between devices with their start and end apart: 9, of which 7 were waited for; matrix products, arithmetic and copies ran while one was open for 0% of the time, Pallas kernels for 18%

profile of v2, /device:TPU:1, one launch (start us, length us, event | category | flops | bytes accessed | tf_op | source)
XLA Modules:
  0.0 112.8 jit_solution(153626615526767626)
XLA Ops:
  0.6 13.5 %grams.1 = (f32[896,128]{1,0:T(8,128)}, f32[896,128]{1,0:T(8,128)}) custom-call(s32[4096]{0:T(1024)} %bitcast.7, s32[1]{0:T(128)} %bitcast.core, f32[4096,128]{1,0:T(8,128)} %refs_0_.1, f32[32,128]{1,0:T(8,128)} %bitcast.10, f32[4,4096,128]{2,1,0:T(8,128)} %bases.5), custom_call_target="tpu_custom_call" | custom-call | tf_op jit(solution)/shard_map/grams/pallas_call | solution.py:163
  14.1 3.2 %collective-permute-start = (f32[896,128]{1,0:T(8,128)}, f32[896,128]{1,0:T(8,128)S(1)}, u32[]{:S(2)}, u32[]{:S(2)}) collective-permute-start(f32[896,128]{1,0:T(8,128)} %get-tuple-element.37), channel_id=1, source_target_pairs={{0,1},{1,0},{2,3},{3,2},{4,5},{5,4},{6,7},{7,6},{8,9},{9,8},{10,11... | collective-permute-start | bytes 1376264 | tf_op jit(solution)/shard_map/ppermute | solution.py:502
  17.4 1.7 %collective-permute-done = f32[896,128]{1,0:T(8,128)S(1)} collective-permute-done((f32[896,128]{1,0:T(8,128)}, f32[896,128]{1,0:T(8,128)S(1)}, u32[]{:S(2)}, u32[]{:S(2)}) %collective-permute-start) | collective-permute-done | bytes 458784 | tf_op jit(solution)/shard_map/ppermute | solution.py:502
  19.0 1.9 %add.3 = f32[896,128]{1,0:T(8,128)} add(f32[896,128]{1,0:T(8,128)} %get-tuple-element.36, f32[896,128]{1,0:T(8,128)S(1)} %collective-permute-done) | non-fusion elementwise | flops 114688 | bytes 1376256 | tf_op jit(solution)/shard_map/add | solution.py:505
  20.9 5.0 %all-to-all-start = ((f32[16,56,128]{2,1,0:T(8,128)}), f32[16,56,128]{2,1,0:T(8,128)S(1)}, u32[]{:S(2)}, u32[]{:S(2)}) async-start(f32[16,56,128]{2,1,0:T(8,128)} %bitcast.3), calls=%async_computation | async-start | bytes 917504 | tf_op jit(solution)/shard_map/all_to_all | solution.py:514
  25.9 11.5 %place.2 = (bf16[4096,128]{1,0:T(8,128)(2,1)S(1)}, bf16[4096,128]{1,0:T(8,128)(2,1)}, bf16[4096,128]{1,0:T(8,128)(2,1)}, bf16[4096,128]{1,0:T(8,128)(2,1)}, f32[4096,128]{1,0:T(8,128)}) custom-call(s32[4096]{0:T(1024)S(1)} %bitcast.8, f32[32,128]{1,0:T(8,128)S(1)} %bitcast.11, f32[4,4096,128]{2,1,0:T(8,128)} %bases.5, f32[4096,128]{1,0:T(8,128)} %refs_0_.1), custom_call_target="tpu_custom_call" | custom-call | flops 20971520 | bytes 11534336 | tf_op jit(solution)/shard_map/place/pallas_call | solution.py:380
  38.3 6.7 %all-to-all-start.1 = ((f32[16,56,128]{2,1,0:T(8,128)}), f32[16,56,128]{2,1,0:T(8,128)S(1)}, u32[]{:S(2)}, u32[]{:S(2)}) async-start(f32[16,56,128]{2,1,0:T(8,128)} %sum_parts.1), calls=%async_computation.1 | async-start | bytes 917504 | tf_op jit(solution)/shard_map/all_to_all | solution.py:514
  44.9 9.2 %place.3 = (bf16[4096,128]{1,0:T(8,128)(2,1)S(1)}, bf16[4096,128]{1,0:T(8,128)(2,1)}, bf16[4096,128]{1,0:T(8,128)(2,1)}, bf16[4096,128]{1,0:T(8,128)(2,1)}) custom-call(s32[4096]{0:T(1024)S(1)} %bitcast.9, f32[32,128]{1,0:T(8,128)S(1)} %bitcast.12, f32[4,4096,128]{2,1,0:T(8,128)} %bases.5), custom_call_target="tpu_custom_call" | custom-call | flops 20971520 | bytes 11534336 | tf_op jit(solution)/shard_map/place/pallas_call | solution.py:380
  54.1 1.1 copy-done
  55.2 1.5 %collective-permute-start.1 = (f32[896,128]{1,0:T(8,128)S(1)}, f32[896,128]{1,0:T(8,128)S(1)}, u32[]{:S(2)}, u32[]{:S(2)}) collective-permute-start(f32[896,128]{1,0:T(8,128)S(1)} %bitcast.5), channel_id=1, source_target_pairs={{0,1},{1,0},{2,3},{3,2},{4,5},{5,4},{6,7},{7,6},{8,9},{9,8},{10,11... | collective-permute-start | bytes 1376264 | tf_op jit(solution)/shard_map/ppermute | solution.py:502
  56.7 1.4 %collective-permute-done.1.refs_1_ = f32[896,128]{1,0:T(8,128)S(1)} collective-permute-done((f32[896,128]{1,0:T(8,128)S(1)}, f32[896,128]{1,0:T(8,128)S(1)}, u32[]{:S(2)}, u32[]{:S(2)}) %collective-permute-start.1) | collective-permute-done | bytes 458784 | tf_op jit(solution)/shard_map/ppermute | solution.py:502
  58.1 3.9 %level.3 = (f32[4,128,128]{2,1,0:T(8,128)S(1)}, f32[1152,128]{1,0:T(8,128)S(1)}, f32[576,128]{1,0:T(8,128)S(1)}) custom-call(s32[1]{0:T(128)} %bitcast.core, f32[896,128]{1,0:T(8,128)S(1)} %bitcast.6, f32[896,128]{1,0:T(8,128)S(1)} %collective-permute-done.1.refs_1_), custom_call_target="tpu_custom_call" | custom-call | tf_op jit(solution)/shard_map/level/pallas_call | solution.py:294
  62.1 1.7 %collective-permute-start.2 = (f32[576,128]{1,0:T(8,128)S(1)}, f32[576,128]{1,0:T(8,128)S(1)}, u32[]{:S(2)}, u32[]{:S(2)}) collective-permute-start(f32[576,128]{1,0:T(8,128)S(1)} %get-tuple-element.54), channel_id=1, source_target_pairs={{0,2},{1,3},{2,0},{3,1},{4,6},{5,7},{6,4},{7,5},{8,10},{9,11},{10,... | collective-permute-start | bytes 884744 | tf_op jit(solution)/shard_map/ppermute | solution.py:502
  63.8 7.0 %collective-permute-done.2.refs_1_ = f32[576,128]{1,0:T(8,128)S(1)} collective-permute-done((f32[576,128]{1,0:T(8,128)S(1)}, f32[576,128]{1,0:T(8,128)S(1)}, u32[]{:S(2)}, u32[]{:S(2)}) %collective-permute-start.2) | collective-permute-done | bytes 294944 | tf_op jit(solution)/shard_map/ppermute | solution.py:502
  70.8 1.0 collective-permute-start.3
  71.8 1.2 %collective-permute-done.3.refs_2_ = f32[576,128]{1,0:T(8,128)S(1)} collective-permute-done((f32[576,128]{1,0:T(8,128)S(1)}, f32[576,128]{1,0:T(8,128)S(1)}, u32[]{:S(2)}, u32[]{:S(2)}) %collective-permute-start.3) | collective-permute-done | bytes 294944 | tf_op jit(solution)/shard_map/ppermute | solution.py:502
  73.0 3.7 %level.4 = (f32[3,128,128]{2,1,0:T(8,128)S(1)}, f32[640,128]{1,0:T(8,128)S(1)}, f32[320,128]{1,0:T(8,128)S(1)}) custom-call(s32[1]{0:T(128)} %bitcast.core, f32[1152,128]{1,0:T(8,128)S(1)} %get-tuple-element.53.refs_0_, f32[576,128]{1,0:T(8,128)S(1)} %collective-permute-done.2.refs_1_, f32[576,128]{1,0:T(8,128)S(1)} %collective-permute-done.3.refs_2_), custom_call_target="tpu_custom_call" | custom-call | tf_op jit(solution)/shard_map/level/pallas_call | solution.py:294
  76.7 3.2 %collective-permute-start.4 = (f32[320,128]{1,0:T(8,128)S(1)}, f32[320,128]{1,0:T(8,128)S(1)}, u32[]{:S(2)}, u32[]{:S(2)}) collective-permute-start(f32[320,128]{1,0:T(8,128)S(1)} %get-tuple-element.56), channel_id=1, source_target_pairs={{0,4},{1,5},{2,6},{3,7},{4,0},{5,1},{6,2},{7,3},{8,12},{9,13},{10,... | collective-permute-start | bytes 491528 | tf_op jit(solution)/shard_map/ppermute | solution.py:502
  80.0 7.8 %collective-permute-done.4.refs_1_ = f32[320,128]{1,0:T(8,128)S(1)} collective-permute-done((f32[320,128]{1,0:T(8,128)S(1)}, f32[320,128]{1,0:T(8,128)S(1)}, u32[]{:S(2)}, u32[]{:S(2)}) %collective-permute-start.4) | collective-permute-done | bytes 163872 | tf_op jit(solution)/shard_map/ppermute | solution.py:502
  88.6 1.0 collective-permute-done.5.refs_2_
  89.7 3.5 %level.5 = (f32[2,128,128]{2,1,0:T(8,128)S(1)}, f32[256,128]{1,0:T(8,128)S(1)}) custom-call(s32[1]{0:T(128)} %bitcast.core, f32[640,128]{1,0:T(8,128)S(1)} %get-tuple-element.55.refs_0_, f32[320,128]{1,0:T(8,128)S(1)} %collective-permute-done.4.refs_1_, f32[320,128]{1,0:T(8,128)S(1)} %collective-permute-done.5.refs_2_), custom_call_target="tpu_custom_call" | custom-call | tf_op jit(solution)/shard_map/level/pallas_call | solution.py:294
  93.2 4.8 %collective-permute-start.6 = (f32[256,128]{1,0:T(8,128)S(1)}, f32[256,128]{1,0:T(8,128)S(1)}, u32[]{:S(2)}, u32[]{:S(2)}) collective-permute-start(f32[256,128]{1,0:T(8,128)S(1)} %get-tuple-element.57.left), channel_id=1, source_target_pairs={{0,14},{1,15},{2,12},{3,13},{4,10},{5,11},{6,8},{7,9},{8,6},{9,7},... | collective-permute-start | bytes 393224 | tf_op jit(solution)/shard_map/ppermute | solution.py:502
  98.1 5.8 %collective-permute-done.6.came = f32[256,128]{1,0:T(8,128)S(1)} collective-permute-done((f32[256,128]{1,0:T(8,128)S(1)}, f32[256,128]{1,0:T(8,128)S(1)}, u32[]{:S(2)}, u32[]{:S(2)}) %collective-permute-start.6) | collective-permute-done | bytes 131104 | tf_op jit(solution)/shard_map/ppermute | solution.py:502
  103.8 8.8 %apply.1 = (f32[4096,128]{1,0:T(8,128)}, f32[4,128,128]{2,1,0:T(8,128)}) custom-call(f32[256,128]{1,0:T(8,128)S(1)} %get-tuple-element.57.left, f32[256,128]{1,0:T(8,128)S(1)} %collective-permute-done.6.came, f32[2,128,128]{2,1,0:T(8,128)S(1)} %get-tuple-element.58.refs_0_, f32[3,128,128]{2,1,0:T(8,128)S(1)} %get-tuple-element.59.refs_1_, ...), custom_call_target="tpu_custom_call" | custom-call | tf_op jit(solution)/shard_map/apply/pallas_call | solution.py:464
  (9 shorter events, 1.7 us)
Async XLA Ops:
  14.1 11.8 %copy-start.1 = (s32[1,4096]{1,0:T(1,128)S(1)}, s32[1,4096]{1,0:T(1,128)}, u32[]{:S(2)}) copy-start(s32[1,4096]{1,0:T(1,128)} %param.4) | copy-start | bytes 49156
  14.1 11.8 %copy-start.2 = (f32[4096]{0:T(1024)S(1)}, f32[4096]{0:T(1024)}, u32[]{:S(2)}) copy-start(f32[4096]{0:T(1024)} %param.6) | copy-start | bytes 49156
  14.1 4.9 %collective-permute-start = (f32[896,128]{1,0:T(8,128)}, f32[896,128]{1,0:T(8,128)S(1)}, u32[]{:S(2)}, u32[]{:S(2)}) collective-permute-start(f32[896,128]{1,0:T(8,128)} %get-tuple-element.37), channel_id=1, source_target_pairs={{0,1},{1,0},{2,3},{3,2},{4,5},{5,4},{6,7},{7,6},{8,9},{9,8},{10,11... | collective-permute-start | bytes 1376264 | tf_op jit(solution)/shard_map/ppermute | solution.py:502
  20.9 16.6 %all-to-all-start = ((f32[16,56,128]{2,1,0:T(8,128)}), f32[16,56,128]{2,1,0:T(8,128)S(1)}, u32[]{:S(2)}, u32[]{:S(2)}) async-start(f32[16,56,128]{2,1,0:T(8,128)} %bitcast.3), calls=%async_computation | async-start | bytes 917504 | tf_op jit(solution)/shard_map/all_to_all | solution.py:514
  38.3 16.9 %all-to-all-start.1 = ((f32[16,56,128]{2,1,0:T(8,128)}), f32[16,56,128]{2,1,0:T(8,128)S(1)}, u32[]{:S(2)}, u32[]{:S(2)}) async-start(f32[16,56,128]{2,1,0:T(8,128)} %sum_parts.1), calls=%async_computation.1 | async-start | bytes 917504 | tf_op jit(solution)/shard_map/all_to_all | solution.py:514
  54.1 1.1 copy-start
  55.2 3.0 %collective-permute-start.1 = (f32[896,128]{1,0:T(8,128)S(1)}, f32[896,128]{1,0:T(8,128)S(1)}, u32[]{:S(2)}, u32[]{:S(2)}) collective-permute-start(f32[896,128]{1,0:T(8,128)S(1)} %bitcast.5), channel_id=1, source_target_pairs={{0,1},{1,0},{2,3},{3,2},{4,5},{5,4},{6,7},{7,6},{8,9},{9,8},{10,11... | collective-permute-start | bytes 1376264 | tf_op jit(solution)/shard_map/ppermute | solution.py:502
  62.1 8.7 %collective-permute-start.2 = (f32[576,128]{1,0:T(8,128)S(1)}, f32[576,128]{1,0:T(8,128)S(1)}, u32[]{:S(2)}, u32[]{:S(2)}) collective-permute-start(f32[576,128]{1,0:T(8,128)S(1)} %get-tuple-element.54), channel_id=1, source_target_pairs={{0,2},{1,3},{2,0},{3,1},{4,6},{5,7},{6,4},{7,5},{8,10},{9,11},{10,... | collective-permute-start | bytes 884744 | tf_op jit(solution)/shard_map/ppermute | solution.py:502
  70.8 2.2 %collective-permute-start.3 = (f32[576,128]{1,0:T(8,128)S(1)}, f32[576,128]{1,0:T(8,128)S(1)}, u32[]{:S(2)}, u32[]{:S(2)}) collective-permute-start(f32[576,128]{1,0:T(8,128)S(1)} %collective-permute-done.2.refs_1_), channel_id=1, source_target_pairs={{0,1},{1,0},{2,3},{3,2},{4,5},{5,4},{6,7},{7,6},{8,9},{9,8},{10,11... | collective-permute-start | bytes 884744 | tf_op jit(solution)/shard_map/ppermute | solution.py:502
  76.7 11.0 %collective-permute-start.4 = (f32[320,128]{1,0:T(8,128)S(1)}, f32[320,128]{1,0:T(8,128)S(1)}, u32[]{:S(2)}, u32[]{:S(2)}) collective-permute-start(f32[320,128]{1,0:T(8,128)S(1)} %get-tuple-element.56), channel_id=1, source_target_pairs={{0,4},{1,5},{2,6},{3,7},{4,0},{5,1},{6,2},{7,3},{8,12},{9,13},{10,... | collective-permute-start | bytes 491528 | tf_op jit(solution)/shard_map/ppermute | solution.py:502
  87.7 1.9 %collective-permute-start.5 = (f32[320,128]{1,0:T(8,128)S(1)}, f32[320,128]{1,0:T(8,128)S(1)}, u32[]{:S(2)}, u32[]{:S(2)}) collective-permute-start(f32[320,128]{1,0:T(8,128)S(1)} %collective-permute-done.4.refs_1_), channel_id=1, source_target_pairs={{0,1},{1,0},{2,3},{3,2},{4,5},{5,4},{6,7},{7,6},{8,9},{9,8},{10,11... | collective-permute-start | bytes 491528 | tf_op jit(solution)/shard_map/ppermute | solution.py:502
  93.2 10.6 %collective-permute-start.6 = (f32[256,128]{1,0:T(8,128)S(1)}, f32[256,128]{1,0:T(8,128)S(1)}, u32[]{:S(2)}, u32[]{:S(2)}) collective-permute-start(f32[256,128]{1,0:T(8,128)S(1)} %get-tuple-element.57.left), channel_id=1, source_target_pairs={{0,14},{1,15},{2,12},{3,13},{4,10},{5,11},{6,8},{7,9},{8,6},{9,7},... | collective-permute-start | bytes 393224 | tf_op jit(solution)/shard_map/ppermute | solution.py:502

commit v3 on v2

--- a/solution.py
+++ b/solution.py
@@ -77,99 +77,109 @@
     return [(k, c) for k in range(levels - 1, -1, -1) for c in range(-1, k + 1)]
 
 
-def gram_kernel(levels, scales, order, core, targets, noise, bases,
-                keep, give, acc, acc_t, whole, gathered):
-    step = pl.program_id(0)
-    tile = bases.shape[1]
+def gram_kernel(levels, scales, core, order_in, noise_in, targets, bases, keep, give,
+                acc, acc_t, whole, gathered, held, given, order, noise, in_sem):
+    points = given.shape[0]
     width = levels * R
-
-    @pl.when(step == 0)
-    def _():
-        acc[...] = jnp.zeros_like(acc)
-        acc_t[...] = jnp.zeros_like(acc_t)
-
-    for row in range(tile):
-        gathered[pl.ds(row, 1), :] = targets[pl.ds(order[step * tile + row], 1), :]
-    root = column(1.0 / jnp.sqrt(noise[pl.ds(step * (tile // R), tile // R), :]))
-    pieces = [split(bases[k] * root) for k in range(levels)]
-    high = jnp.concatenate([p[0] for p in pieces], axis=1)
-    low = jnp.concatenate([p[1] for p in pieces], axis=1)
-    right_h, right_l = split(gathered[...] * root)
-    turned = high.T
-    every = jnp.concatenate([high, low, right_h, right_l], axis=1)
-    near = width // 2
-    acc[0:near, 0:near] += dot16(turned[0:near, :], high[:, 0:near])
-    acc[:, near:] += dot16(turned, every[:, near:])
-    acc_t[...] += dot16(right_h.T, low)
-
-    @pl.when(step == pl.num_programs(0) - 1)
-    def _():
-        blocks = block_list(levels)
-        half = len(blocks) // 2
-        for at, (k, c) in enumerate(blocks):
-            rows = block(k)
-            if c < 0:
-                value = (
-                    acc[rows, block(2 * levels)]
-                    + acc[rows, block(2 * levels + 1)]
-                    + acc_t[:, block(k)].T
-                ) * scales[k]
-            else:
-                same = acc[rows, block(c)]
-                if c < levels // 2 <= k:
-                    same = acc[block(c), rows].T
-                value = (
-                    same
-                    + acc[rows, block(levels + c)]
-                    + acc[block(c), block(levels + k)].T
-                ) * (scales[k] * scales[c])
-            whole[block(at), :] = value
-        rows = half * R
-
-        @pl.when(core[0] == 0)
+    tiles = points // TILE
+
+    def load(t, k):
+        rows = pl.ds(pl.multiple_of(t * TILE, TILE), TILE)
+        return pltpu.make_async_copy(
+            bases.at[k, rows, :], held.at[k, rows, :], in_sem.at[t, k]
+        )
+
+    early = [
+        pltpu.make_async_copy(noise_in, noise, in_sem.at[1, levels]),
+        pltpu.make_async_copy(order_in, order, in_sem.at[2, levels]),
+        pltpu.make_async_copy(targets, given, in_sem.at[0, levels]),
+    ]
+    for copy in early:
+        copy.start()
+    for t in range(tiles):
+        for k in range(levels):
+            load(t, k).start()
+    acc[...] = jnp.zeros_like(acc)
+    acc_t[...] = jnp.zeros_like(acc_t)
+    for copy in early:
+        copy.wait()
+
+    def some(t, _):
+        for k in range(levels):
+            load(t, k).wait()
+        rows = pl.ds(pl.multiple_of(t * TILE, TILE), TILE)
+        for row in range(TILE):
+            gathered[pl.ds(row, 1), :] = given[pl.ds(order[t * TILE + row], 1), :]
+        lines = TILE // R
+        root = column(1.0 / jnp.sqrt(noise[pl.ds(pl.multiple_of(t * lines, lines), lines), :]))
+        pieces = [split(held[k, rows, :] * root) for k in range(levels)]
+        high = jnp.concatenate([p[0] for p in pieces], axis=1)
+        low = jnp.concatenate([p[1] for p in pieces], axis=1)
+        right_h, right_l = split(gathered[...] * root)
+        turned = high.T
+        every = jnp.concatenate([high, low, right_h, right_l], axis=1)
+        near = width // 2
+        acc[0:near, 0:near] += dot16(turned[0:near, :], high[:, 0:near])
+        acc[:, near:] += dot16(turned, every[:, near:])
+        acc_t[...] += dot16(right_h.T, low)
+        return 0
+
+    lax.fori_loop(0, tiles, some, 0)
+    blocks = block_list(levels)
+    half = len(blocks) // 2
+    for at, (k, c) in enumerate(blocks):
+        rows = block(k)
+        if c < 0:
+            value = (
+                acc[rows, block(2 * levels)]
+                + acc[rows, block(2 * levels + 1)]
+                + acc_t[:, block(k)].T
+            ) * scales[k]
+        else:
+            same = acc[rows, block(c)]
+            if c < levels // 2 <= k:
+                same = acc[block(c), rows].T
+            value = (
+                same
+                + acc[rows, block(levels + c)]
+                + acc[block(c), block(levels + k)].T
+            ) * (scales[k] * scales[c])
+        whole[block(at), :] = value
+    rows = half * R
+    for first in (0, 1):
+
+        @pl.when(core[0] == first)
         def _():
-            keep[...] = whole[0:rows, :]
-            give[...] = whole[rows : 2 * rows, :]
-
-        @pl.when(core[0] != 0)
-        def _():
-            give[...] = whole[0:rows, :]
-            keep[...] = whole[rows : 2 * rows, :]
+            keep[...] = whole[first * rows : (first + 1) * rows, :]
+            give[...] = whole[(1 - first) * rows : (2 - first) * rows, :]
 
 
 def grams(order, core, targets, noise, bases, scales):
     levels, points, _ = bases.shape
     half = len(block_list(levels)) // 2 * R
     width = levels * R
-    grid_spec = pltpu.PrefetchScalarGridSpec(
-        num_scalar_prefetch=2,
-        grid=(points // TILE,),
-        in_specs=[
-            pl.BlockSpec((points, R), lambda i, *_: (0, 0)),
-            pl.BlockSpec((points // R, R), lambda i, *_: (0, 0)),
-            pl.BlockSpec((levels, TILE, R), lambda i, *_: (0, i, 0)),
-        ],
-        out_specs=[
-            pl.BlockSpec((half, R), lambda i, *_: (0, 0)),
-            pl.BlockSpec((half, R), lambda i, *_: (0, 0)),
-        ],
+    smem = pl.BlockSpec(memory_space=pltpu.SMEM)
+    vmem = pl.BlockSpec(memory_space=pltpu.VMEM)
+    hbm = pl.BlockSpec(memory_space=pltpu.HBM)
+    return pl.pallas_call(
+        functools.partial(gram_kernel, levels, scales),
+        in_specs=[smem] + [hbm] * 4,
+        out_specs=[vmem, vmem],
+        out_shape=[jax.ShapeDtypeStruct((half, R), F32)] * 2,
         scratch_shapes=[
             pltpu.VMEM((width, 2 * width + 2 * R), F32),
             pltpu.VMEM((R, width), F32),
             pltpu.VMEM((2 * half, R), F32),
             pltpu.VMEM((TILE, R), F32),
+            pltpu.VMEM((levels, points, R), F32),
+            pltpu.VMEM((points, R), F32),
+            pltpu.SMEM((points,), jnp.int32),
+            pltpu.VMEM((points // R, R), F32),
+            pltpu.SemaphoreType.DMA((points // TILE, levels + 1)),
         ],
-    )
-    return pl.pallas_call(
-        functools.partial(gram_kernel, levels, scales),
-        grid_spec=grid_spec,
-        out_shape=[
-            jax.ShapeDtypeStruct((half, R), F32),
-            jax.ShapeDtypeStruct((half, R), F32),
-        ],
-        compiler_params=pltpu.CompilerParams(vmem_limit_bytes=56 * MIB),
+        compiler_params=pltpu.CompilerParams(vmem_limit_bytes=52 * MIB),
         name="grams",
-    )(order, core, targets, noise, bases)
+    )(core, order, noise, targets, bases)
 
 
 def sum_kernel(copies, parts, out):
@@ -314,17 +324,19 @@
     lax.fori_loop(0, count // 64, some, 0)
 
 
-def place_kernel(levels, with_base, order, noise, bases, *refs):
+def place_kernel(levels, with_base, order_in, noise_in, bases, *refs):
     count = len(levels)
     if with_base:
         targets, refs = refs[0], refs[1:]
     outs, refs = refs[: 2 * count], refs[2 * count :]
     if with_base:
         base, refs = refs[0], refs[1:]
-    held, placed, made, in_sem, out_sem, *refs = refs
+    if count:
+        held, placed, made, *refs = refs
     if with_base:
-        root, spread, given, based = refs
-    points = held.shape[1]
+        root, spread, given, based, *refs = refs
+    order, noise, in_sem, out_sem = refs
+    points = order.shape[0]
     tiles = points // TILE
 
     def load(t, k):
@@ -339,12 +351,20 @@
             return pltpu.make_async_copy(based.at[rows, :], base.at[rows, :], out_sem.at[t, i])
         return pltpu.make_async_copy(made.at[i, rows, :], outs[i].at[rows, :], out_sem.at[t, i])
 
+    early = [
+        pltpu.make_async_copy(noise_in, noise, in_sem.at[1, count]),
+        pltpu.make_async_copy(order_in, order, in_sem.at[2, count]),
+    ]
+    for copy in early:
+        copy.start()
     for t in range(tiles):
         for k in range(count):
             load(t, k).start()
     if with_base:
         late = pltpu.make_async_copy(targets, given, in_sem.at[0, count])
         late.start()
+    for copy in early:
+        copy.wait()
     for t in range(tiles):
         rows = pl.ds(t * TILE, TILE)
         over = column(1.0 / noise[pl.ds(t * (TILE // R), TILE // R), :])
@@ -375,26 +395,27 @@
     points = order.shape[0]
     count, tiles = len(levels), points // TILE
     with_base = targets is not None
-    anywhere = pl.BlockSpec(memory_space=pl.ANY)
+    hbm = pl.BlockSpec(memory_space=pltpu.HBM)
     one = pltpu.VMEM((points, R), F32)
     return pl.pallas_call(
         functools.partial(place_kernel, levels, with_base),
-        in_specs=[
-            pl.BlockSpec(memory_space=pltpu.SMEM),
-            pl.BlockSpec(memory_space=pltpu.VMEM),
-        ]
-        + [anywhere] * (1 + with_base),
-        out_specs=[anywhere] * (2 * count + with_base),
+        in_specs=[hbm] * (3 + with_base),
+        out_specs=[hbm] * (2 * count + with_base),
         out_shape=[jax.ShapeDtypeStruct((points, R), BF16)] * (2 * count)
         + [jax.ShapeDtypeStruct((points, R), F32)] * with_base,
         scratch_shapes=[
             pltpu.VMEM((count, points, R), F32),
             pltpu.VMEM((count, points, R), F32),
             pltpu.VMEM((2 * count, points, R), BF16),
+        ]
+        * (count > 0)
+        + [one] * (4 * with_base)
+        + [
+            pltpu.SMEM((points,), jnp.int32),
+            pltpu.VMEM((points // R, R), F32),
             pltpu.SemaphoreType.DMA((tiles, count + 1)),
             pltpu.SemaphoreType.DMA((tiles, 2 * count + 1)),
-        ]
-        + [one] * (4 * with_base),
+        ],
         compiler_params=pltpu.CompilerParams(vmem_limit_bytes=52 * MIB),
         cost_estimate=pl.CostEstimate(
             flops=points * R * 40, bytes_accessed=11 * MIB, transcendentals=0
@@ -460,11 +481,11 @@
     levels = len(scales)
     tiles = points // TILE
     vmem = pl.BlockSpec(memory_space=pltpu.VMEM)
-    anywhere = pl.BlockSpec(memory_space=pl.ANY)
+    hbm = pl.BlockSpec(memory_space=pltpu.HBM)
     return pl.pallas_call(
         functools.partial(apply_kernel, levels, scales),
-        in_specs=[vmem] * (len(incoming) + len(weights)) + [anywhere] * (len(placed) + 1),
-        out_specs=[anywhere, vmem],
+        in_specs=[vmem] * (len(incoming) + len(weights)) + [hbm] * (len(placed) + 1),
+        out_specs=[hbm, vmem],
         out_shape=[
             jax.ShapeDtypeStruct((points, R), F32),
             jax.ShapeDtypeStruct((levels, R, R), F32),
@@ -513,11 +534,8 @@
 
     spread = lambda a: lax.all_to_all(a, ("y", "x"), 0, 0)
     half = levels // 2
-    parts, (*placed, base) = beside(
-        mine.reshape(plane, -1, R), spread, list(range(half)), targets
-    )
-    parts, more = beside(sum_and_copy(parts), spread, list(range(half, levels)))
-    placed += more
+    parts, placed = beside(mine.reshape(plane, -1, R), spread, list(range(half)))
+    parts = spread(sum_and_copy(parts))
     mine = parts.reshape(-1, R)
     incoming = (mine, swap(mine, 0, 1))
     weights = []
@@ -525,9 +543,12 @@
         found, left, *give = solve_level(level, core, incoming)
         weights.insert(0, found)
         if give:
-            came = swap(give[0], 1 << (levels - 1 - level), 0)
+            move = lambda a: swap(a, 1 << (levels - 1 - level), 0)
+            came, more = beside(give[0], move, [half - 1 + len(weights)])
+            placed += more
             incoming = (left, came, swap(came, 0, 1))
-    came = swap(left, sizes["z"] - 1, 0)
+    move = lambda a: swap(a, sizes["z"] - 1, 0)
+    came, (base,) = beside(left, move, [], targets)
     return tuple(apply((left, came), weights, placed, base, scales))
 
 

time: 113 us -> 108 us (0.956)
  waiting for transfers between devices: 25.9 us -> 7.57 us
  blocking collectives: 0 us -> 14.5 us
  starting transfers between devices: 28.1 us -> 22.5 us
  Pallas kernels: 55 us -> 59.1 us
  local copies, waits for them, and re-layouts: 1.06 us -> 2.42 us
    ppermute x7, waiting for transfers between devices: 25.9 us -> 6.03 us  [swap(): return lax.ppermute(value, axes, [(i, i ^ flip) for i in range(count)])]
    all_to_all x0 -> x1, blocking collectives: none -> 14.5 us  [on_device(): spread = lambda a: lax.all_to_all(a, ('y', 'x'), 0, 0)]
    pallas_call x2 -> x4, Pallas kernels: 20.7 us -> 28.1 us  [place(): pl.pallas_call(functools.partial(place_kernel, levels, with_base), in_spe...]
    all_to_all x2 -> x1, starting transfers between devices: 11.7 us -> 5.02 us  [on_device(): spread = lambda a: lax.all_to_all(a, ('y', 'x'), 0, 0)]
    pallas_call x1, Pallas kernels: 13.5 us -> 11.6 us  [grams(): pl.pallas_call(functools.partial(gram_kernel, levels, scales), in_specs=[...]
    all_to_all x2 -> x1, waiting for transfers between devices: 0.01 us -> 1.54 us  [on_device(): spread = lambda a: lax.all_to_all(a, ('y', 'x'), 0, 0)]
    unnamed x6 -> x12, local copies, waits for them, and re-layouts: 1.06 us -> 2.42 us
  transfers between devices with their start and end apart: 9 -> 8, of which waited for: 7 -> 6; matrix products, arithmetic and copies ran while one was open for 0% -> 0% of each run, Pallas kernels for 18% -> 26%
where the time goes in v3:
time: 108 us
  Pallas kernels  59.1 us (55%)
  starting transfers between devices  22.5 us (21%)
  blocking collectives  14.5 us (13%)
  waiting for transfers between devices  7.57 us (7%)
  local copies, waits for them, and re-layouts  2.42 us (2%)
    pallas_call x4, Pallas kernels, place(): pl.pallas_call(functools.partial(place_kernel, levels, with_base), in_spe...  28.1 us
    ppermute x7, starting transfers between devices, swap(): return lax.ppermute(value, axes, [(i, i ^ flip) for i in range(count)])  17.5 us
    all_to_all x1, blocking collectives, on_device(): spread = lambda a: lax.all_to_all(a, ('y', 'x'), 0, 0)  14.5 us
    pallas_call x1, Pallas kernels, grams(): pl.pallas_call(functools.partial(gram_kernel, levels, scales), in_specs=[...  11.6 us
    pallas_call x3, Pallas kernels, solve_level(): pl.pallas_call(functools.partial(level_kernel, level, first), in_specs=[s...  10.5 us
    pallas_call x1, Pallas kernels, apply(): pl.pallas_call(functools.partial(apply_kernel, levels, scales), in_specs=...  8.82 us
    ppermute x7, waiting for transfers between devices, swap(): return lax.ppermute(value, axes, [(i, i ^ flip) for i in range(count)])  6.03 us
    all_to_all x1, starting transfers between devices, on_device(): spread = lambda a: lax.all_to_all(a, ('y', 'x'), 0, 0)  5.02 us
  transfers between devices with their start and end apart: 8, of which 6 were waited for; matrix products, arithmetic and copies ran while one was open for 0% of the time, Pallas kernels for 26%

profile of v3, /device:TPU:1, one launch (start us, length us, event | category | flops | bytes accessed | tf_op | source)
XLA Modules:
  0.0 107.9 jit_solution(12492264363060083371)
XLA Ops:
  2.1 11.6 %grams.1 = (f32[896,128]{1,0:T(8,128)S(1)}, f32[896,128]{1,0:T(8,128)S(1)}) custom-call(s32[1]{0:T(128)} %bitcast.core, s32[4096]{0:T(1024)S(1)} %bitcast.7, f32[32,128]{1,0:T(8,128)S(1)} %bitcast.12, f32[4096,128]{1,0:T(8,128)} %refs_0_.1, f32[4,4096,128]{2,1,0:T(8,128)} %bases.9), custom_call_target="tpu_custom_call" | custom-call | tf_op jit(solution)/shard_map/grams/pallas_call | solution.py:164
  13.7 3.3 %collective-permute-start = (f32[896,128]{1,0:T(8,128)S(1)}, f32[896,128]{1,0:T(8,128)S(1)}, u32[]{:S(2)}, u32[]{:S(2)}) collective-permute-start(f32[896,128]{1,0:T(8,128)S(1)} %get-tuple-element.42), channel_id=1, source_target_pairs={{0,1},{1,0},{2,3},{3,2},{4,5},{5,4},{6,7},{7,6},{8,9},{9,8},{10,11... | collective-permute-start | bytes 1376264 | tf_op jit(solution)/shard_map/ppermute | solution.py:523
  17.0 1.4 %collective-permute-done = f32[896,128]{1,0:T(8,128)S(1)} collective-permute-done((f32[896,128]{1,0:T(8,128)S(1)}, f32[896,128]{1,0:T(8,128)S(1)}, u32[]{:S(2)}, u32[]{:S(2)}) %collective-permute-start) | collective-permute-done | bytes 458784 | tf_op jit(solution)/shard_map/ppermute | solution.py:523
  19.3 5.0 %all-to-all-start = ((f32[16,56,128]{2,1,0:T(8,128)}), f32[16,56,128]{2,1,0:T(8,128)S(1)}, u32[]{:S(2)}, u32[]{:S(2)}) async-start(f32[16,56,128]{2,1,0:T(8,128)} %bitcast.3), calls=%async_computation | async-start | bytes 917504 | tf_op jit(solution)/shard_map/all_to_all | solution.py:535
  24.3 8.4 %place.4 = (bf16[4096,128]{1,0:T(8,128)(2,1)S(1)}, bf16[4096,128]{1,0:T(8,128)(2,1)}, bf16[4096,128]{1,0:T(8,128)(2,1)}, bf16[4096,128]{1,0:T(8,128)(2,1)}) custom-call(s32[4096]{0:T(1024)S(1)} %bitcast.8, f32[32,128]{1,0:T(8,128)S(1)} %bitcast.13, f32[4,4096,128]{2,1,0:T(8,128)} %bases.9), custom_call_target="tpu_custom_call" | custom-call | flops 20971520 | bytes 11534336 | tf_op jit(solution)/shard_map/place/pallas_call | solution.py:400
  32.7 1.5 %all-to-all-done.parts = f32[16,56,128]{2,1,0:T(8,128)S(1)} async-done(((f32[16,56,128]{2,1,0:T(8,128)}), f32[16,56,128]{2,1,0:T(8,128)S(1)}, u32[]{:S(2)}, u32[]{:S(2)}) %all-to-all-start) | async-done | bytes 458784 | tf_op jit(solution)/shard_map/all_to_all | solution.py:535
  34.3 14.5 %all_to_all.10 = f32[16,56,128]{2,1,0:T(8,128)S(1)} all-to-all(f32[16,56,128]{2,1,0:T(8,128)S(1)} %sum_parts.1), channel_id=1, replica_groups=mesh['y'=4,'x'=4,'z'=8,'c'=2] {'y','x'}, dimensions={0} | all-to-all | bytes 917504 | tf_op jit(solution)/shard_map/all_to_all | solution.py:535
  48.8 2.1 %collective-permute-start.1 = (f32[896,128]{1,0:T(8,128)S(1)}, f32[896,128]{1,0:T(8,128)S(1)}, u32[]{:S(2)}, u32[]{:S(2)}) collective-permute-start(f32[896,128]{1,0:T(8,128)S(1)} %bitcast.5), channel_id=1, source_target_pairs={{0,1},{1,0},{2,3},{3,2},{4,5},{5,4},{6,7},{7,6},{8,9},{9,8},{10,11... | collective-permute-start | bytes 1376264 | tf_op jit(solution)/shard_map/ppermute | solution.py:523
  51.0 1.4 %collective-permute-done.1.refs_1_ = f32[896,128]{1,0:T(8,128)S(1)} collective-permute-done((f32[896,128]{1,0:T(8,128)S(1)}, f32[896,128]{1,0:T(8,128)S(1)}, u32[]{:S(2)}, u32[]{:S(2)}) %collective-permute-start.1) | collective-permute-done | bytes 458784 | tf_op jit(solution)/shard_map/ppermute | solution.py:523
  52.4 3.6 %level.3 = (f32[4,128,128]{2,1,0:T(8,128)S(1)}, f32[1152,128]{1,0:T(8,128)S(1)}, f32[576,128]{1,0:T(8,128)S(1)}) custom-call(s32[1]{0:T(128)} %bitcast.core, f32[896,128]{1,0:T(8,128)S(1)} %bitcast.6, f32[896,128]{1,0:T(8,128)S(1)} %collective-permute-done.1.refs_1_), custom_call_target="tpu_custom_call" | custom-call | tf_op jit(solution)/shard_map/level/pallas_call | solution.py:304
  56.0 2.1 %collective-permute-start.2 = (f32[576,128]{1,0:T(8,128)S(1)}, f32[576,128]{1,0:T(8,128)S(1)}, u32[]{:S(2)}, u32[]{:S(2)}) collective-permute-start(f32[576,128]{1,0:T(8,128)S(1)} %get-tuple-element.52), channel_id=1, source_target_pairs={{0,2},{1,3},{2,0},{3,1},{4,6},{5,7},{6,4},{7,5},{8,10},{9,11},{10,... | collective-permute-start | bytes 884744 | tf_op jit(solution)/shard_map/ppermute | solution.py:523
  58.1 6.6 %place.5 = (bf16[4096,128]{1,0:T(8,128)(2,1)S(1)}, bf16[4096,128]{1,0:T(8,128)(2,1)}) custom-call(s32[4096]{0:T(1024)S(1)} %bitcast.9, f32[32,128]{1,0:T(8,128)S(1)} %bitcast.14, f32[4,4096,128]{2,1,0:T(8,128)} %bases.9), custom_call_target="tpu_custom_call" | custom-call | flops 20971520 | bytes 11534336 | tf_op jit(solution)/shard_map/place/pallas_call | solution.py:400
  64.7 1.0 copy-done
  66.3 1.2 %collective-permute-done.3.refs_2_ = f32[576,128]{1,0:T(8,128)S(1)} collective-permute-done((f32[576,128]{1,0:T(8,128)S(1)}, f32[576,128]{1,0:T(8,128)S(1)}, u32[]{:S(2)}, u32[]{:S(2)}) %collective-permute-start.3) | collective-permute-done | bytes 294944 | tf_op jit(solution)/shard_map/ppermute | solution.py:523
  67.5 3.7 %level.4 = (f32[3,128,128]{2,1,0:T(8,128)S(1)}, f32[640,128]{1,0:T(8,128)S(1)}, f32[320,128]{1,0:T(8,128)S(1)}) custom-call(s32[1]{0:T(128)} %bitcast.core, f32[1152,128]{1,0:T(8,128)S(1)} %get-tuple-element.50.refs_0_, f32[576,128]{1,0:T(8,128)S(1)} %collective-permute-done.2.refs_1_, f32[576,128]{1,0:T(8,128)S(1)} %collective-permute-done.3.refs_2_), custom_call_target="tpu_custom_call" | custom-call | tf_op jit(solution)/shard_map/level/pallas_call | solution.py:304
  71.3 2.6 %collective-permute-start.4 = (f32[320,128]{1,0:T(8,128)S(1)}, f32[320,128]{1,0:T(8,128)S(1)}, u32[]{:S(2)}, u32[]{:S(2)}) collective-permute-start(f32[320,128]{1,0:T(8,128)S(1)} %get-tuple-element.59), channel_id=1, source_target_pairs={{0,4},{1,5},{2,6},{3,7},{4,0},{5,1},{6,2},{7,3},{8,12},{9,13},{10,... | collective-permute-start | bytes 491528 | tf_op jit(solution)/shard_map/ppermute | solution.py:523
  73.8 6.6 %place.6 = (bf16[4096,128]{1,0:T(8,128)(2,1)S(1)}, bf16[4096,128]{1,0:T(8,128)(2,1)}) custom-call(s32[4096]{0:T(1024)S(1)} %bitcast.10, f32[32,128]{1,0:T(8,128)S(1)} %bitcast.15, f32[4,4096,128]{2,1,0:T(8,128)} %bases.9), custom_call_target="tpu_custom_call" | custom-call | flops 20971520 | bytes 11534336 | tf_op jit(solution)/shard_map/place/pallas_call | solution.py:400
  80.5 0.9 collective-permute-done.4.refs_1_
  81.4 1.2 %collective-permute-start.5 = (f32[320,128]{1,0:T(8,128)S(1)}, f32[320,128]{1,0:T(8,128)S(1)}, u32[]{:S(2)}, u32[]{:S(2)}) collective-permute-start(f32[320,128]{1,0:T(8,128)S(1)} %collective-permute-done.4.refs_1_), channel_id=1, source_target_pairs={{0,1},{1,0},{2,3},{3,2},{4,5},{5,4},{6,7},{7,6},{8,9},{9,8},{10,11... | collective-permute-start | bytes 491528 | tf_op jit(solution)/shard_map/ppermute | solution.py:523
  82.6 1.0 collective-permute-done.5.refs_2_
  83.6 3.2 %level.5 = (f32[2,128,128]{2,1,0:T(8,128)S(1)}, f32[256,128]{1,0:T(8,128)S(1)}) custom-call(s32[1]{0:T(128)} %bitcast.core, f32[640,128]{1,0:T(8,128)S(1)} %get-tuple-element.57.refs_0_, f32[320,128]{1,0:T(8,128)S(1)} %collective-permute-done.4.refs_1_, f32[320,128]{1,0:T(8,128)S(1)} %collective-permute-done.5.refs_2_), custom_call_target="tpu_custom_call" | custom-call | tf_op jit(solution)/shard_map/level/pallas_call | solution.py:304
  86.8 5.6 %collective-permute-start.6 = (f32[256,128]{1,0:T(8,128)S(1)}, f32[256,128]{1,0:T(8,128)S(1)}, u32[]{:S(2)}, u32[]{:S(2)}) collective-permute-start(f32[256,128]{1,0:T(8,128)S(1)} %get-tuple-element.65.left), channel_id=1, source_target_pairs={{0,14},{1,15},{2,12},{3,13},{4,10},{5,11},{6,8},{7,9},{8,6},{9,7},... | collective-permute-start | bytes 393224 | tf_op jit(solution)/shard_map/ppermute | solution.py:523
  92.4 6.5 %place.7.refs_11_ = f32[4096,128]{1,0:T(8,128)} custom-call(s32[4096]{0:T(1024)S(1)} %bitcast.11, f32[32,128]{1,0:T(8,128)S(1)} %bitcast.16, f32[4,4096,128]{2,1,0:T(8,128)} %bases.9, f32[4096,128]{1,0:T(8,128)} %refs_0_.1), custom_call_target="tpu_custom_call" | custom-call | flops 20971520 | bytes 11534336 | tf_op jit(solution)/shard_map/place/pallas_call | solution.py:400
  98.9 8.8 %apply.1 = (f32[4096,128]{1,0:T(8,128)}, f32[4,128,128]{2,1,0:T(8,128)}) custom-call(f32[256,128]{1,0:T(8,128)S(1)} %get-tuple-element.65.left, f32[256,128]{1,0:T(8,128)S(1)} %collective-permute-done.6.came, f32[2,128,128]{2,1,0:T(8,128)S(1)} %get-tuple-element.68.refs_0_, f32[3,128,128]{2,1,0:T(8,128)S(1)} %get-tuple-element.69.refs_1_, ...), custom_call_target="tpu_custom_call" | custom-call | tf_op jit(solution)/shard_map/apply/pallas_call | solution.py:485
  (16 shorter events, 3.0 us)
Async XLA Ops:
  0.6 0.7 copy-start.2
  1.4 0.7 copy-start.4
  13.7 10.6 %copy-start.3 = (s32[1,4096]{1,0:T(1,128)S(1)}, s32[1,4096]{1,0:T(1,128)}, u32[]{:S(2)}) copy-start(s32[1,4096]{1,0:T(1,128)} %param.4) | copy-start | bytes 49156
  13.7 10.6 %copy-start.5 = (f32[4096]{0:T(1024)S(1)}, f32[4096]{0:T(1024)}, u32[]{:S(2)}) copy-start(f32[4096]{0:T(1024)} %param.6) | copy-start | bytes 49156
  13.7 4.8 %collective-permute-start = (f32[896,128]{1,0:T(8,128)S(1)}, f32[896,128]{1,0:T(8,128)S(1)}, u32[]{:S(2)}, u32[]{:S(2)}) collective-permute-start(f32[896,128]{1,0:T(8,128)S(1)} %get-tuple-element.42), channel_id=1, source_target_pairs={{0,1},{1,0},{2,3},{3,2},{4,5},{5,4},{6,7},{7,6},{8,9},{9,8},{10,11... | collective-permute-start | bytes 1376264 | tf_op jit(solution)/shard_map/ppermute | solution.py:523
  19.3 14.9 %all-to-all-start = ((f32[16,56,128]{2,1,0:T(8,128)}), f32[16,56,128]{2,1,0:T(8,128)S(1)}, u32[]{:S(2)}, u32[]{:S(2)}) async-start(f32[16,56,128]{2,1,0:T(8,128)} %bitcast.3), calls=%async_computation | async-start | bytes 917504 | tf_op jit(solution)/shard_map/all_to_all | solution.py:535
  48.8 3.6 %collective-permute-start.1 = (f32[896,128]{1,0:T(8,128)S(1)}, f32[896,128]{1,0:T(8,128)S(1)}, u32[]{:S(2)}, u32[]{:S(2)}) collective-permute-start(f32[896,128]{1,0:T(8,128)S(1)} %bitcast.5), channel_id=1, source_target_pairs={{0,1},{1,0},{2,3},{3,2},{4,5},{5,4},{6,7},{7,6},{8,9},{9,8},{10,11... | collective-permute-start | bytes 1376264 | tf_op jit(solution)/shard_map/ppermute | solution.py:523
  56.0 9.6 %collective-permute-start.2 = (f32[576,128]{1,0:T(8,128)S(1)}, f32[576,128]{1,0:T(8,128)S(1)}, u32[]{:S(2)}, u32[]{:S(2)}) collective-permute-start(f32[576,128]{1,0:T(8,128)S(1)} %get-tuple-element.52), channel_id=1, source_target_pairs={{0,2},{1,3},{2,0},{3,1},{4,6},{5,7},{6,4},{7,5},{8,10},{9,11},{10,... | collective-permute-start | bytes 884744 | tf_op jit(solution)/shard_map/ppermute | solution.py:523
  64.7 1.0 copy-start
  65.6 1.9 %collective-permute-start.3 = (f32[576,128]{1,0:T(8,128)S(1)}, f32[576,128]{1,0:T(8,128)S(1)}, u32[]{:S(2)}, u32[]{:S(2)}) collective-permute-start(f32[576,128]{1,0:T(8,128)S(1)} %collective-permute-done.2.refs_1_), channel_id=1, source_target_pairs={{0,1},{1,0},{2,3},{3,2},{4,5},{5,4},{6,7},{7,6},{8,9},{9,8},{10,11... | collective-permute-start | bytes 884744 | tf_op jit(solution)/shard_map/ppermute | solution.py:523
  71.3 10.1 %collective-permute-start.4 = (f32[320,128]{1,0:T(8,128)S(1)}, f32[320,128]{1,0:T(8,128)S(1)}, u32[]{:S(2)}, u32[]{:S(2)}) collective-permute-start(f32[320,128]{1,0:T(8,128)S(1)} %get-tuple-element.59), channel_id=1, source_target_pairs={{0,4},{1,5},{2,6},{3,7},{4,0},{5,1},{6,2},{7,3},{8,12},{9,13},{10,... | collective-permute-start | bytes 491528 | tf_op jit(solution)/shard_map/ppermute | solution.py:523
  80.4 18.5 %copy-start.1 = (bf16[4096,128]{1,0:T(8,128)(2,1)}, bf16[4096,128]{1,0:T(8,128)(2,1)S(1)}, u32[]{:S(2)}) copy-start(bf16[4096,128]{1,0:T(8,128)(2,1)S(1)} %get-tuple-element.77.refs_9_) | copy-start | bytes 3145732
  81.4 2.2 %collective-permute-start.5 = (f32[320,128]{1,0:T(8,128)S(1)}, f32[320,128]{1,0:T(8,128)S(1)}, u32[]{:S(2)}, u32[]{:S(2)}) collective-permute-start(f32[320,128]{1,0:T(8,128)S(1)} %collective-permute-done.4.refs_1_), channel_id=1, source_target_pairs={{0,1},{1,0},{2,3},{3,2},{4,5},{5,4},{6,7},{7,6},{8,9},{9,8},{10,11... | collective-permute-start | bytes 491528 | tf_op jit(solution)/shard_map/ppermute | solution.py:523
  86.8 12.1 %collective-permute-start.6 = (f32[256,128]{1,0:T(8,128)S(1)}, f32[256,128]{1,0:T(8,128)S(1)}, u32[]{:S(2)}, u32[]{:S(2)}) collective-permute-start(f32[256,128]{1,0:T(8,128)S(1)} %get-tuple-element.65.left), channel_id=1, source_target_pairs={{0,14},{1,15},{2,12},{3,13},{4,10},{5,11},{6,8},{7,9},{8,6},{9,7},... | collective-permute-start | bytes 393224 | tf_op jit(solution)/shard_map/ppermute | solution.py:523

commit v4 on v3

--- a/solution.py
+++ b/solution.py
@@ -21,16 +21,6 @@
     return a1, a2, (rest - a2.astype(F32)).astype(BF16)
 
 
-def left3(a):
-    a1, a2 = split(a)
-    return jnp.concatenate([a1, a1, a2], axis=1)
-
-
-def right3(b):
-    b1, b2 = split(b)
-    return jnp.concatenate([b1, b2, b1], axis=0)
-
-
 def left6(a):
     a1, a2, a3 = three(a)
     return jnp.concatenate([a1, a1, a2, a1, a3, a2], axis=1)
@@ -39,10 +29,6 @@
 def right6(b):
     b1, b2, b3 = three(b)
     return jnp.concatenate([b1, b2, b1, b3, b1, b2], axis=0)
-
-
-def dot3(a, b):
-    return dot16(left3(a), right3(b))
 
 
 def dot(a, b):
@@ -190,37 +176,40 @@
         out[i] = total
 
 
-def sum_and_copy(parts):
+def sum_and_copy(parts, copies):
     return pl.pallas_call(
-        functools.partial(sum_kernel, parts.shape[0]),
-        out_shape=jax.ShapeDtypeStruct(parts.shape, F32),
+        functools.partial(sum_kernel, copies),
+        out_shape=jax.ShapeDtypeStruct((copies, *parts.shape[1:]), F32),
         compiler_params=pltpu.CompilerParams(vmem_limit_bytes=8 * MIB),
         name="sum_parts",
     )(parts)
 
 
-def inverse(c, power, result):
-    n = c.shape[0]
+def inverses(several, power, result):
+    n = several[0].shape[0]
     on_diagonal = lax.broadcasted_iota(jnp.int32, (n, n), 0) == lax.broadcasted_iota(
         jnp.int32, (n, n), 1
     )
     eye = jnp.where(on_diagonal, 1.0, 0.0).astype(F32)
-    diagonal = jnp.sum(c * eye, axis=0, keepdims=True)
-    radius = jnp.sum(jnp.abs(c), axis=0, keepdims=True) - jnp.abs(diagonal)
-    top = jnp.max(diagonal + radius)
-    low = jnp.maximum(jnp.min(diagonal - radius), 1.0)
-    factor = 2.0 / (low + top)
-    bound = (top - low) / (low + top)
-    power[...] = eye - factor * c
-    result[...] = factor * (eye + power[...])
+    bound = jnp.float32(0.0)
+    for i, c in enumerate(several):
+        diagonal = jnp.sum(c * eye, axis=0, keepdims=True)
+        radius = jnp.sum(jnp.abs(c), axis=0, keepdims=True) - jnp.abs(diagonal)
+        top = jnp.max(diagonal + radius)
+        low = jnp.maximum(jnp.min(diagonal - radius), 1.0)
+        factor = 2.0 / (low + top)
+        bound = jnp.maximum(bound, (top - low) / (low + top))
+        power[i] = eye - factor * c
+        result[i] = factor * (eye + power[i])
 
     def cond(bound):
         return bound > 1e-4
 
     def body(bound):
-        e = dot3(power[...], power[...])
-        power[...] = e
-        result[...] += dot3(result[...], e)
+        for i in range(len(several)):
+            e = dot(power[i], power[i])
+            power[i] = e
+            result[i] += dot(result[i], e)
         return bound * bound
 
     lax.while_loop(cond, body, bound * bound)
@@ -229,13 +218,16 @@
         return jnp.logical_and(state[0] > 1e-4, state[1] < 8)
 
     def body_r(state):
-        x = result[...]
-        residual = eye - dot(c, x)
-        result[...] = x + dot3(x, residual)
-        return jnp.max(jnp.abs(residual)), state[1] + 1
+        worst = jnp.float32(0.0)
+        for i, c in enumerate(several):
+            x = result[i]
+            residual = eye - dot(c, x)
+            result[i] = x + dot(x, residual)
+            worst = jnp.maximum(worst, jnp.max(jnp.abs(residual)))
+        return worst, state[1] + 1
 
     lax.while_loop(cond_r, body_r, (jnp.float32(1.0), jnp.int32(0)))
-    return result[...]
+    return [result[i] for i in range(len(several))]
 
 
 def capacitance(own):
@@ -248,7 +240,7 @@
 
 def eliminate(level, total, weights, left, give, core, power, result):
     get = lambda i: total[block(i), :]
-    inv = left6(inverse(capacitance(get(level + 1)), power, result))
+    inv = left6(inverses([capacitance(get(level + 1))], power, result)[0])
     found = []
     for i in range(level + 1):
         value = dot16(inv, right6(get(i)))
@@ -258,8 +250,6 @@
         if col < 0:
             turned = left6(get(k + 1).T)
         left[block(i), :] = get(level + 2 + i) - dot16(turned, found[col + 1])
-    if give is None:
-        return
     size = give.shape[0]
 
     @pl.when(core[0] == 0)
@@ -284,29 +274,63 @@
                 total[place : place + half, :] = value
 
 
-def level_kernel(level, first, core, *refs):
-    refs = list(refs)
-    before = None if first else refs.pop(0)
-    mine, other, weights, left, *give, total, power, result = refs
-    join(core, total, mine, other, before)
-    eliminate(level, total, weights, left, give[0] if give else None, core, power, result)
-
-
-def solve_level(level, core, incoming):
-    first = len(incoming) == 2
-    after = len(block_list(level))
+def pair_kernel(level, core, which, mine, other, weights, above, left, give,
+                total, middle, power, result):
+    get = lambda p, i: total[p, block(i), :]
+    for p in (0, 1):
+        join(core, total.at[p], mine.at[p], other.at[p])
+    own = [capacitance(get(p, level + 1)) for p in (0, 1)]
+    inv = [left6(x) for x in inverses(own, power, result)]
+    found = [[], []]
+    for i in range(level + 1):
+        values = [dot16(inv[p], right6(get(p, i))) for p in (0, 1)]
+        weights[i] = jnp.where(which[0] == 0, values[0], values[1])
+        for p in (0, 1):
+            found[p].append(right6(values[p]))
+    for i, (k, col) in enumerate(block_list(level)):
+        if col < 0:
+            turned = [left6(get(p, k + 1).T) for p in (0, 1)]
+        parts = [get(p, level + 2 + i) - dot16(turned[p], found[p][col + 1]) for p in (0, 1)]
+        middle[block(i), :] = parts[0] + parts[1]
+    eliminate(level - 1, middle, above, left, give, core, power, result)
+
+
+def solve_pair(level, core, which, mine, other):
+    after = len(block_list(level - 1)) * R
     smem = pl.BlockSpec(memory_space=pltpu.SMEM)
     vmem = pl.BlockSpec(memory_space=pltpu.VMEM)
-    rows = 2 * incoming[-1].shape[0]
-    shapes = [(level + 1, R, R), (after * R, R)]
-    if level > 1:
-        shapes.append((after * R // 2, R))
+    shapes = [(level + 1, R, R), (level, R, R), (after, R), (after // 2, R)]
     return pl.pallas_call(
-        functools.partial(level_kernel, level, first),
-        in_specs=[smem] + [vmem] * len(incoming),
-        out_specs=[vmem] * len(shapes),
+        functools.partial(pair_kernel, level),
+        in_specs=[smem, smem, vmem, vmem],
+        out_specs=[vmem] * 4,
         out_shape=[jax.ShapeDtypeStruct(shape, F32) for shape in shapes],
-        scratch_shapes=[pltpu.VMEM((rows, R), F32)] + [pltpu.VMEM((R, R), F32)] * 2,
+        scratch_shapes=[
+            pltpu.VMEM((2, 2 * mine.shape[1], R), F32),
+            pltpu.VMEM((len(block_list(level)) * R, R), F32),
+        ]
+        + [pltpu.VMEM((2, R, R), F32)] * 2,
+        compiler_params=pltpu.CompilerParams(vmem_limit_bytes=16 * MIB),
+        name="pair",
+    )(core, which, mine, other)
+
+
+def level_kernel(level, core, before, mine, other, weights, left, give, total, power, result):
+    join(core, total, mine, other, before)
+    eliminate(level, total, weights, left, give, core, power, result)
+
+
+def solve_level(level, core, incoming):
+    after = len(block_list(level)) * R
+    smem = pl.BlockSpec(memory_space=pltpu.SMEM)
+    vmem = pl.BlockSpec(memory_space=pltpu.VMEM)
+    shapes = [(level + 1, R, R), (after, R), (after // 2, R)]
+    return pl.pallas_call(
+        functools.partial(level_kernel, level),
+        in_specs=[smem] + [vmem] * 3,
+        out_specs=[vmem] * 3,
+        out_shape=[jax.ShapeDtypeStruct(shape, F32) for shape in shapes],
+        scratch_shapes=[pltpu.VMEM(incoming[0].shape, F32)] + [pltpu.VMEM((1, R, R), F32)] * 2,
         compiler_params=pltpu.CompilerParams(vmem_limit_bytes=12 * MIB),
         name="level",
     )(core, *incoming)
@@ -424,10 +448,36 @@
     )(order, noise, bases, *([targets] if with_base else []))
 
 
-def apply_kernel(levels, scales, left, came, *refs):
-    weights, refs = refs[: levels - 1], refs[levels - 1 :]
+def chain_kernel(*refs):
+    *weights, plain, slope = refs
+    for k, w in enumerate(weights):
+        value, factor = w[0], -w[1]
+        for j in range(k):
+            left = left6(w[j + 2])
+            value = value - dot16(left, right6(plain[j]))
+            factor = factor - dot16(left, right6(slope[j]))
+        plain[k] = value
+        slope[k] = factor
+
+
+def chain(weights):
+    count = len(weights)
+    return pl.pallas_call(
+        chain_kernel,
+        out_shape=[jax.ShapeDtypeStruct((count, R, R), F32)] * 2,
+        compiler_params=pltpu.CompilerParams(vmem_limit_bytes=8 * MIB),
+        cost_estimate=pl.CostEstimate(
+            flops=40 * 2 * R**3, bytes_accessed=20 * 4 * R * R, transcendentals=0
+        ),
+        name="chain",
+    )(*weights)
+
+
+def apply_kernel(levels, scales, core, before, mine, other, *refs):
+    weights, (plain, slope), refs = refs[: levels - 1], refs[levels - 1 : levels + 1], refs[levels + 1 :]
     given, refs = refs[: 2 * levels + 1], refs[2 * levels + 1 :]
-    solved, node_weights, highs, lows, base, out, coefs, power, result, in_sem, out_sem = refs
+    solved, node_weights, highs, lows, base, out, coefs, total, power, result, *refs = refs
+    in_sem, out_sem = refs
     points = base.shape[0]
     tiles = points // TILE
 
@@ -449,17 +499,15 @@
     for t in range(tiles):
         for copy in copies(t):
             copy.start()
-    total = left[...] + came[...]
-    inv = inverse(capacitance(total[R:, :]), power, result)
-    found = [dot(inv, total[:R, :])]
-    node_weights[0] = found[0]
+    join(core, total, mine, other, before)
+    inv = inverses([capacitance(total[R:, :])], power, result)[0]
+    root = dot(inv, total[:R, :])
+    node_weights[0] = root
+    found = [root]
+    root = right6(root)
     for k in range(1, levels):
-        w = weights[k - 1]
-        value = w[0]
-        node_weights[k] = value
-        for j in range(k):
-            value = value - dot(w[j + 1], found[j])
-        found.append(value)
+        node_weights[k] = weights[k - 1][0]
+        found.append(plain[k - 1] + dot16(left6(slope[k - 1]), root))
     for k in range(levels):
         h, l = split(found[k] * scales[k])
         coefs[block(k), 0:R] = h
@@ -476,7 +524,7 @@
         write(t).wait()
 
 
-def apply(incoming, weights, placed, base, scales):
+def apply(core, incoming, weights, chained, placed, base, scales):
     points = base.shape[0]
     levels = len(scales)
     tiles = points // TILE
@@ -484,7 +532,9 @@
     hbm = pl.BlockSpec(memory_space=pltpu.HBM)
     return pl.pallas_call(
         functools.partial(apply_kernel, levels, scales),
-        in_specs=[vmem] * (len(incoming) + len(weights)) + [hbm] * (len(placed) + 1),
+        in_specs=[pl.BlockSpec(memory_space=pltpu.SMEM)]
+        + [vmem] * (len(incoming) + len(weights) + 2)
+        + [hbm] * (len(placed) + 1),
         out_specs=[hbm, vmem],
         out_shape=[
             jax.ShapeDtypeStruct((points, R), F32),
@@ -496,29 +546,32 @@
             pltpu.VMEM((points, R), F32),
             pltpu.VMEM((points, R), F32),
             pltpu.VMEM((levels * R, 2 * R), BF16),
-            pltpu.VMEM((R, R), F32),
-            pltpu.VMEM((R, R), F32),
+            pltpu.VMEM((2 * R, R), F32),
+            pltpu.VMEM((1, R, R), F32),
+            pltpu.VMEM((1, R, R), F32),
             pltpu.SemaphoreType.DMA((tiles, 2 * levels + 1)),
             pltpu.SemaphoreType.DMA((tiles,)),
         ],
         compiler_params=pltpu.CompilerParams(vmem_limit_bytes=52 * MIB),
         name="apply",
-    )(*incoming, *weights, *placed, base)
+    )(core, *incoming, *weights, *chained, *placed, base)
 
 
 def on_device(tree_order, targets, noise_var, node_bases):
     levels, points, _ = node_bases.shape
-    sizes = {a: lax.axis_size(a) for a in ("y", "x", "z", "c")}
-    axes = ("y", "x", "z", "c")
+    axes = ("y", "x", "quad", "pair", "c")
+    sizes = {a: lax.axis_size(a) for a in axes}
     plane = sizes["y"] * sizes["x"]
-    all_points = points * plane * sizes["z"] * sizes["c"]
+    planes = sizes["quad"] * sizes["pair"]
+    all_points = points * plane * planes * sizes["c"]
     scales = [float(all_points / 2**k) ** -0.5 for k in range(levels)]
     order = tree_order[0]
     core = lax.axis_index("c").astype(jnp.int32).reshape(1)
+    which = lax.axis_index("pair").astype(jnp.int32).reshape(1)
     noise = noise_var.reshape(points // R, R)
 
     def swap(value, z_bit, c_bit):
-        count = plane * sizes["z"] * sizes["c"]
+        count = plane * planes * sizes["c"]
         flip = z_bit * sizes["c"] + c_bit
         return lax.ppermute(value, axes, [(i, i ^ flip) for i in range(count)])
 
@@ -532,31 +585,34 @@
         value, *made = lax.optimization_barrier((value, *made))
         return value, made
 
-    spread = lambda a: lax.all_to_all(a, ("y", "x"), 0, 0)
     half = levels // 2
-    parts, placed = beside(mine.reshape(plane, -1, R), spread, list(range(half)))
-    parts = spread(sum_and_copy(parts))
-    mine = parts.reshape(-1, R)
-    incoming = (mine, swap(mine, 0, 1))
-    weights = []
-    for level in range(levels - 1, 0, -1):
-        found, left, *give = solve_level(level, core, incoming)
-        weights.insert(0, found)
-        if give:
-            move = lambda a: swap(a, 1 << (levels - 1 - level), 0)
-            came, more = beside(give[0], move, [half - 1 + len(weights)])
-            placed += more
-            incoming = (left, came, swap(came, 0, 1))
-    move = lambda a: swap(a, sizes["z"] - 1, 0)
-    came, (base,) = beside(left, move, [], targets)
-    return tuple(apply((left, came), weights, placed, base, scales))
+    parts, placed = beside(
+        mine.reshape(plane, -1, R),
+        lambda a: lax.all_to_all(a, ("y", "x"), 0, 0),
+        list(range(half)),
+    )
+    parts, more = beside(
+        sum_and_copy(parts, 2 * plane),
+        lambda a: lax.all_to_all(a, ("pair", "y", "x"), 0, 0),
+        list(range(half, levels)),
+    )
+    placed += more
+    mine = parts.reshape(2, -1, R)
+    first, second, left, give = solve_pair(levels - 1, core, which, mine, swap(mine, 0, 1))
+    came, (base,) = beside(give, lambda a: swap(a, 2, 0), [], targets)
+    third, left, give = solve_level(1, core, (left, came, swap(came, 0, 1)))
+    came = swap(give, planes - 1, 0)
+    weights = [third, second, first]
+    chained = chain(weights)
+    incoming = (left, came, swap(came, 0, 1))
+    return tuple(apply(core, incoming, weights, chained, placed, base, scales))
 
 
 def solution(mesh):
-    fine = Mesh(mesh.devices.reshape(4, 4, 8, 2), ("y", "x", "z", "c"))
-    points = ("z", "c", "y", "x")
+    fine = Mesh(mesh.devices.reshape(4, 4, 4, 2, 2), ("y", "x", "quad", "pair", "c"))
+    points = ("quad", "pair", "c", "y", "x")
     in_specs = (P(points, None), P(points, None), P(points), P(None, points, None))
-    out_specs = (P(points, None), P(("z", "c"), None, None))
+    out_specs = (P(points, None), P(("quad", "pair", "c"), None, None))
     return jax.shard_map(
         on_device, mesh=fine, in_specs=in_specs, out_specs=out_specs, check_vma=False
     )

time: 108 us -> 108 us (level); the launches traced: 108 us -> 107 us
  blocking collectives: 14.5 us -> 0 us
  waiting for transfers between devices: 7.57 us -> 14.6 us
  starting transfers between devices: 22.5 us -> 27.9 us
    all_to_all x1 -> x0, blocking collectives: 14.5 us -> none  [on_device(): spread = lambda a: lax.all_to_all(a, ('y', 'x'), 0, 0)]
    all_to_all x1 -> x2, starting transfers between devices: 5.02 us -> 12.8 us  [the longest x1 7.76 us: on_device(): lax.all_to_all(a, ('pair', 'y', 'x'), 0, 0)]
    pallas_call x4, Pallas kernels: 10.6 us -> 15.6 us  [the longest x1 10.4 us: solve_pair(): pl.pallas_call(functools.partial(pair_kernel, level), in_specs=[smem, sme...]
    pallas_call x4 -> x3, Pallas kernels: 28.1 us -> 23.3 us  [place(): pl.pallas_call(functools.partial(place_kernel, levels, with_base), in_spe...]
    ppermute x7 -> x6, waiting for transfers between devices: 6.03 us -> 10.1 us  [swap(): return lax.ppermute(value, axes, [(i, i ^ flip) for i in range(count)])]
    all_to_all x1 -> x2, waiting for transfers between devices: 1.54 us -> 4.52 us  [the longest x1 3.96 us: on_device(): lax.all_to_all(a, ('pair', 'y', 'x'), 0, 0)]
    ppermute x7 -> x6, starting transfers between devices: 17.5 us -> 15.1 us  [swap(): return lax.ppermute(value, axes, [(i, i ^ flip) for i in range(count)])]
  transfers between devices with their start and end apart: 8 -> 8, of which waited for: 6 -> 8; matrix products, arithmetic and copies ran while one was open for 0% -> 0% of each run, Pallas kernels for 26% -> 22%
where the time goes in v4:
time: 108 us; the launch traced here: 107 us
  Pallas kernels  59.1 us (55%)
  starting transfers between devices  27.9 us (26%)
  waiting for transfers between devices  14.6 us (14%)
  local copies, waits for them, and re-layouts  3.41 us (3%)
    pallas_call x3, Pallas kernels, place(): pl.pallas_call(functools.partial(place_kernel, levels, with_base), in_spe...  23.3 us
    ppermute x6, starting transfers between devices, swap(): return lax.ppermute(value, axes, [(i, i ^ flip) for i in range(count)])  15.1 us
    pallas_call x1, Pallas kernels, grams(): pl.pallas_call(functools.partial(gram_kernel, levels, scales), in_specs=[...  11.6 us
    pallas_call x1, Pallas kernels, solve_pair(): pl.pallas_call(functools.partial(pair_kernel, level), in_specs=[smem, sme...  10.4 us
    ppermute x6, waiting for transfers between devices, swap(): return lax.ppermute(value, axes, [(i, i ^ flip) for i in range(count)])  10.1 us
    pallas_call x1, Pallas kernels, apply(): pl.pallas_call(functools.partial(apply_kernel, levels, scales), in_specs=...  8.58 us
    all_to_all x1, starting transfers between devices, on_device(): lax.all_to_all(a, ('pair', 'y', 'x'), 0, 0)  7.76 us
    all_to_all x1, starting transfers between devices, on_device(): lax.all_to_all(a, ('y', 'x'), 0, 0)  4.99 us
  transfers between devices with their start and end apart: 8, of which 8 were waited for; matrix products, arithmetic and copies ran while one was open for 0% of the time, Pallas kernels for 22%

profile of v4, /device:TPU:1, one launch (start us, length us, event | category | flops | bytes accessed | tf_op | source)
XLA Modules:
  0.0 106.8 jit_solution(6614704264014003433)
XLA Ops:
  2.1 11.6 %grams.1 = (f32[896,128]{1,0:T(8,128)S(1)}, f32[896,128]{1,0:T(8,128)S(1)}) custom-call(s32[1]{0:T(128)} %bitcast.core, s32[4096]{0:T(1024)S(1)} %bitcast.8, f32[32,128]{1,0:T(8,128)S(1)} %bitcast.12, f32[4096,128]{1,0:T(8,128)} %refs_0_.1, f32[4,4096,128]{2,1,0:T(8,128)} %bases.7), custom_call_target="tpu_custom_call" | custom-call | tf_op jit(solution)/shard_map/grams/pallas_call | solution.py:150
  13.7 3.3 %collective-permute-start = (f32[896,128]{1,0:T(8,128)S(1)}, f32[896,128]{1,0:T(8,128)S(1)}, u32[]{:S(2)}, u32[]{:S(2)}) collective-permute-start(f32[896,128]{1,0:T(8,128)S(1)} %get-tuple-element.40), channel_id=1, source_target_pairs={{0,1},{1,0},{2,3},{3,2},{4,5},{5,4},{6,7},{7,6},{8,9},{9,8},{10,11... | collective-permute-start | bytes 1376264 | tf_op jit(solution)/shard_map/ppermute | solution.py:576
  17.1 1.4 %collective-permute-done = f32[896,128]{1,0:T(8,128)S(1)} collective-permute-done((f32[896,128]{1,0:T(8,128)S(1)}, f32[896,128]{1,0:T(8,128)S(1)}, u32[]{:S(2)}, u32[]{:S(2)}) %collective-permute-start) | collective-permute-done | bytes 458784 | tf_op jit(solution)/shard_map/ppermute | solution.py:576
  18.5 0.8 add.3
  19.3 5.0 %all-to-all-start = ((f32[16,56,128]{2,1,0:T(8,128)}), f32[16,56,128]{2,1,0:T(8,128)S(1)}, u32[]{:S(2)}, u32[]{:S(2)}) async-start(f32[16,56,128]{2,1,0:T(8,128)} %bitcast.4), calls=%async_computation | async-start | bytes 917504 | tf_op jit(solution)/shard_map/all_to_all | solution.py:591
  24.3 8.4 %place.3 = (bf16[4096,128]{1,0:T(8,128)(2,1)S(1)}, bf16[4096,128]{1,0:T(8,128)(2,1)}, bf16[4096,128]{1,0:T(8,128)(2,1)}, bf16[4096,128]{1,0:T(8,128)(2,1)}) custom-call(s32[4096]{0:T(1024)S(1)} %bitcast.9, f32[32,128]{1,0:T(8,128)S(1)} %bitcast.13, f32[4,4096,128]{2,1,0:T(8,128)} %bases.7), custom_call_target="tpu_custom_call" | custom-call | flops 20971520 | bytes 11534336 | tf_op jit(solution)/shard_map/place/pallas_call | solution.py:424
  32.7 1.0 copy-done
  34.2 1.0 sum_parts.1
  35.2 7.8 %all-to-all-start.1 = ((f32[32,56,128]{2,1,0:T(8,128)}), f32[32,56,128]{2,1,0:T(8,128)S(1)}, u32[]{:S(2)}, u32[]{:S(2)}) async-start(f32[32,56,128]{2,1,0:T(8,128)} %sum_parts.1), calls=%async_computation.1 | async-start | bytes 1835008 | tf_op jit(solution)/shard_map/all_to_all | solution.py:596
  43.0 8.4 %place.4 = (bf16[4096,128]{1,0:T(8,128)(2,1)S(1)}, bf16[4096,128]{1,0:T(8,128)(2,1)}, bf16[4096,128]{1,0:T(8,128)(2,1)}, bf16[4096,128]{1,0:T(8,128)(2,1)}) custom-call(s32[4096]{0:T(1024)S(1)} %bitcast.10, f32[32,128]{1,0:T(8,128)S(1)} %bitcast.14, f32[4,4096,128]{2,1,0:T(8,128)} %bases.7), custom_call_target="tpu_custom_call" | custom-call | flops 20971520 | bytes 11534336 | tf_op jit(solution)/shard_map/place/pallas_call | solution.py:424
  51.4 1.0 copy-done.1
  52.4 4.0 %all-to-all-done.1 = f32[32,56,128]{2,1,0:T(8,128)S(1)} async-done(((f32[32,56,128]{2,1,0:T(8,128)}), f32[32,56,128]{2,1,0:T(8,128)S(1)}, u32[]{:S(2)}, u32[]{:S(2)}) %all-to-all-start.1) | async-done | bytes 917536 | tf_op jit(solution)/shard_map/all_to_all | solution.py:596
  56.4 3.1 %collective-permute-start.1 = (f32[2,896,128]{2,1,0:T(8,128)S(1)}, f32[2,896,128]{2,1,0:T(8,128)S(1)}, u32[]{:S(2)}, u32[]{:S(2)}) collective-permute-start(f32[2,896,128]{2,1,0:T(8,128)S(1)} %bitcast.6), channel_id=1, source_target_pairs={{0,1},{1,0},{2,3},{3,2},{4,5},{5,4},{6,7},{7,6},{8,9},{9,8},{10,11... | collective-permute-start | bytes 2752520 | tf_op jit(solution)/shard_map/ppermute | solution.py:576
  59.5 2.1 %collective-permute-done.1.other = f32[2,896,128]{2,1,0:T(8,128)S(1)} collective-permute-done((f32[2,896,128]{2,1,0:T(8,128)S(1)}, f32[2,896,128]{2,1,0:T(8,128)S(1)}, u32[]{:S(2)}, u32[]{:S(2)}) %collective-permute-start.1) | collective-permute-done | bytes 917536 | tf_op jit(solution)/shard_map/ppermute | solution.py:576
  61.6 10.4 %pair.1 = (f32[4,128,128]{2,1,0:T(8,128)S(1)}, f32[3,128,128]{2,1,0:T(8,128)S(1)}, f32[640,128]{1,0:T(8,128)S(1)}, f32[320,128]{1,0:T(8,128)S(1)}) custom-call(s32[1]{0:T(128)} %bitcast.core, s32[1]{0:T(128)} %bitcast.1.which, f32[2,896,128]{2,1,0:T(8,128)S(1)} %bitcast.7, f32[2,896,128]{2,1,0:T(8,128)S(1)} %collective-permute-done.1.other), custom_call_target="tpu_custom_call" | custom-call | tf_op jit(solution)/shard_map/pair/pallas_call | solution.py:303
  72.0 3.7 %collective-permute-start.2 = (f32[320,128]{1,0:T(8,128)S(1)}, f32[320,128]{1,0:T(8,128)S(1)}, u32[]{:S(2)}, u32[]{:S(2)}) collective-permute-start(f32[320,128]{1,0:T(8,128)S(1)} %get-tuple-element.57), channel_id=1, source_target_pairs={{0,4},{1,5},{2,6},{3,7},{4,0},{5,1},{6,2},{7,3},{8,12},{9,13},{10,... | collective-permute-start | bytes 491528 | tf_op jit(solution)/shard_map/ppermute | solution.py:576
  75.7 6.5 %place.5.refs_13_ = f32[4096,128]{1,0:T(8,128)} custom-call(s32[4096]{0:T(1024)S(1)} %bitcast.11, f32[32,128]{1,0:T(8,128)S(1)} %bitcast.15, f32[4,4096,128]{2,1,0:T(8,128)} %bases.7, f32[4096,128]{1,0:T(8,128)} %refs_0_.1), custom_call_target="tpu_custom_call" | custom-call | flops 20971520 | bytes 11534336 | tf_op jit(solution)/shard_map/place/pallas_call | solution.py:424
  82.3 1.2 %collective-permute-done.2.mine = f32[320,128]{1,0:T(8,128)S(1)} collective-permute-done((f32[320,128]{1,0:T(8,128)S(1)}, f32[320,128]{1,0:T(8,128)S(1)}, u32[]{:S(2)}, u32[]{:S(2)}) %collective-permute-start.2) | collective-permute-done | bytes 163872 | tf_op jit(solution)/shard_map/ppermute | solution.py:576
  83.5 0.9 collective-permute-start.3
  84.4 1.0 collective-permute-done.3.other
  85.4 3.7 %level.1 = (f32[2,128,128]{2,1,0:T(8,128)S(1)}, f32[256,128]{1,0:T(8,128)S(1)}, f32[128,128]{1,0:T(8,128)S(1)}) custom-call(s32[1]{0:T(128)} %bitcast.core, f32[640,128]{1,0:T(8,128)S(1)} %get-tuple-element.55.before, f32[320,128]{1,0:T(8,128)S(1)} %collective-permute-done.2.mine, f32[320,128]{1,0:T(8,128)S(1)} %collective-permute-done.3.other), custom_call_target="tpu_custom_call" | custom-call | tf_op jit(solution)/shard_map/level/pallas_call | solution.py:328
  89.2 3.6 %collective-permute-start.4 = (f32[128,128]{1,0:T(8,128)S(1)}, f32[128,128]{1,0:T(8,128)S(1)}, u32[]{:S(2)}, u32[]{:S(2)}) collective-permute-start(f32[128,128]{1,0:T(8,128)S(1)} %get-tuple-element.61), channel_id=1, source_target_pairs={{0,14},{1,15},{2,12},{3,13},{4,10},{5,11},{6,8},{7,9},{8,6},{9,7},... | collective-permute-start | bytes 196616 | tf_op jit(solution)/shard_map/ppermute | solution.py:576
  92.8 3.9 %collective-permute-done.4.mine = f32[128,128]{1,0:T(8,128)S(1)} collective-permute-done((f32[128,128]{1,0:T(8,128)S(1)}, f32[128,128]{1,0:T(8,128)S(1)}, u32[]{:S(2)}, u32[]{:S(2)}) %collective-permute-start.4) | collective-permute-done | bytes 65568 | tf_op jit(solution)/shard_map/ppermute | solution.py:576
  98.0 8.6 %apply.1 = (f32[4096,128]{1,0:T(8,128)}, f32[4,128,128]{2,1,0:T(8,128)}) custom-call(s32[1]{0:T(128)} %bitcast.core, f32[256,128]{1,0:T(8,128)S(1)} %get-tuple-element.60.before, f32[128,128]{1,0:T(8,128)S(1)} %collective-permute-done.4.mine, f32[128,128]{1,0:T(8,128)S(1)} %collective-permute-done.5.other, f32[2,128,128]{2,1,0:T(8,128)S(1)} %get-tuple-element.62.refs_0_, ...), custom_call_target="tpu_custom_call" | custom-call | tf_op jit(solution)/shard_map/apply/pallas_call | solution.py:533
  (14 shorter events, 3.3 us)
Async XLA Ops:
  0.6 0.7 copy-start.2
  1.4 0.7 copy-start.4
  13.7 10.6 %copy-start.3 = (s32[1,4096]{1,0:T(1,128)S(1)}, s32[1,4096]{1,0:T(1,128)}, u32[]{:S(2)}) copy-start(s32[1,4096]{1,0:T(1,128)} %param.4) | copy-start | bytes 49156
  13.7 10.6 %copy-start.5 = (f32[4096]{0:T(1024)S(1)}, f32[4096]{0:T(1024)}, u32[]{:S(2)}) copy-start(f32[4096]{0:T(1024)} %param.6) | copy-start | bytes 49156
  13.7 4.8 %collective-permute-start = (f32[896,128]{1,0:T(8,128)S(1)}, f32[896,128]{1,0:T(8,128)S(1)}, u32[]{:S(2)}, u32[]{:S(2)}) collective-permute-start(f32[896,128]{1,0:T(8,128)S(1)} %get-tuple-element.40), channel_id=1, source_target_pairs={{0,1},{1,0},{2,3},{3,2},{4,5},{5,4},{6,7},{7,6},{8,9},{9,8},{10,11... | collective-permute-start | bytes 1376264 | tf_op jit(solution)/shard_map/ppermute | solution.py:576
  19.3 14.9 %all-to-all-start = ((f32[16,56,128]{2,1,0:T(8,128)}), f32[16,56,128]{2,1,0:T(8,128)S(1)}, u32[]{:S(2)}, u32[]{:S(2)}) async-start(f32[16,56,128]{2,1,0:T(8,128)} %bitcast.4), calls=%async_computation | async-start | bytes 917504 | tf_op jit(solution)/shard_map/all_to_all | solution.py:591
  32.7 1.0 copy-start
  35.2 21.2 %all-to-all-start.1 = ((f32[32,56,128]{2,1,0:T(8,128)}), f32[32,56,128]{2,1,0:T(8,128)S(1)}, u32[]{:S(2)}, u32[]{:S(2)}) async-start(f32[32,56,128]{2,1,0:T(8,128)} %sum_parts.1), calls=%async_computation.1 | async-start | bytes 1835008 | tf_op jit(solution)/shard_map/all_to_all | solution.py:596
  51.4 1.0 copy-start.1
  56.4 5.2 %collective-permute-start.1 = (f32[2,896,128]{2,1,0:T(8,128)S(1)}, f32[2,896,128]{2,1,0:T(8,128)S(1)}, u32[]{:S(2)}, u32[]{:S(2)}) collective-permute-start(f32[2,896,128]{2,1,0:T(8,128)S(1)} %bitcast.6), channel_id=1, source_target_pairs={{0,1},{1,0},{2,3},{3,2},{4,5},{5,4},{6,7},{7,6},{8,9},{9,8},{10,11... | collective-permute-start | bytes 2752520 | tf_op jit(solution)/shard_map/ppermute | solution.py:576
  72.0 11.5 %collective-permute-start.2 = (f32[320,128]{1,0:T(8,128)S(1)}, f32[320,128]{1,0:T(8,128)S(1)}, u32[]{:S(2)}, u32[]{:S(2)}) collective-permute-start(f32[320,128]{1,0:T(8,128)S(1)} %get-tuple-element.57), channel_id=1, source_target_pairs={{0,4},{1,5},{2,6},{3,7},{4,0},{5,1},{6,2},{7,3},{8,12},{9,13},{10,... | collective-permute-start | bytes 491528 | tf_op jit(solution)/shard_map/ppermute | solution.py:576
  83.5 1.9 %collective-permute-start.3 = (f32[320,128]{1,0:T(8,128)S(1)}, f32[320,128]{1,0:T(8,128)S(1)}, u32[]{:S(2)}, u32[]{:S(2)}) collective-permute-start(f32[320,128]{1,0:T(8,128)S(1)} %collective-permute-done.2.mine), channel_id=1, source_target_pairs={{0,1},{1,0},{2,3},{3,2},{4,5},{5,4},{6,7},{7,6},{8,9},{9,8},{10,11... | collective-permute-start | bytes 491528 | tf_op jit(solution)/shard_map/ppermute | solution.py:576
  89.2 7.5 %collective-permute-start.4 = (f32[128,128]{1,0:T(8,128)S(1)}, f32[128,128]{1,0:T(8,128)S(1)}, u32[]{:S(2)}, u32[]{:S(2)}) collective-permute-start(f32[128,128]{1,0:T(8,128)S(1)} %get-tuple-element.61), channel_id=1, source_target_pairs={{0,14},{1,15},{2,12},{3,13},{4,10},{5,11},{6,8},{7,9},{8,6},{9,7},... | collective-permute-start | bytes 196616 | tf_op jit(solution)/shard_map/ppermute | solution.py:576
  96.7 1.4 %collective-permute-start.5 = (f32[128,128]{1,0:T(8,128)S(1)}, f32[128,128]{1,0:T(8,128)S(1)}, u32[]{:S(2)}, u32[]{:S(2)}) collective-permute-start(f32[128,128]{1,0:T(8,128)S(1)} %collective-permute-done.4.mine), channel_id=1, source_target_pairs={{0,1},{1,0},{2,3},{3,2},{4,5},{5,4},{6,7},{7,6},{8,9},{9,8},{10,11... | collective-permute-start | bytes 196616 | tf_op jit(solution)/shard_map/ppermute | solution.py:576

commit v5 on v4

--- a/solution.py
+++ b/solution.py
@@ -238,18 +238,23 @@
     return jnp.where(on_diagonal, 1.0, 0.0).astype(F32) + 0.5 * (own + own.T)
 
 
+def row_of(get, count):
+    return jnp.concatenate([get(i) for i in range(count)], axis=1)
+
+
 def eliminate(level, total, weights, left, give, core, power, result):
     get = lambda i: total[block(i), :]
     inv = left6(inverses([capacitance(get(level + 1))], power, result)[0])
-    found = []
+    found = dot16(inv, right6(row_of(get, level + 1)))
     for i in range(level + 1):
-        value = dot16(inv, right6(get(i)))
-        weights[i] = value
-        found.append(right6(value))
-    for i, (k, col) in enumerate(block_list(level)):
-        if col < 0:
-            turned = left6(get(k + 1).T)
-        left[block(i), :] = get(level + 2 + i) - dot16(turned, found[col + 1])
+        weights[i] = found[:, i * R : (i + 1) * R]
+    found = right6(found)
+    at = 0
+    for k in range(level - 1, -1, -1):
+        change = dot16(left6(get(k + 1).T), found[:, : (k + 2) * R])
+        for i in range(k + 2):
+            left[block(at), :] = get(level + 2 + at) - change[:, i * R : (i + 1) * R]
+            at += 1
     size = give.shape[0]
 
     @pl.when(core[0] == 0)
@@ -281,17 +286,19 @@
         join(core, total.at[p], mine.at[p], other.at[p])
     own = [capacitance(get(p, level + 1)) for p in (0, 1)]
     inv = [left6(x) for x in inverses(own, power, result)]
-    found = [[], []]
+    found = [dot16(inv[p], right6(row_of(lambda i: get(p, i), level + 1))) for p in (0, 1)]
     for i in range(level + 1):
-        values = [dot16(inv[p], right6(get(p, i))) for p in (0, 1)]
-        weights[i] = jnp.where(which[0] == 0, values[0], values[1])
-        for p in (0, 1):
-            found[p].append(right6(values[p]))
-    for i, (k, col) in enumerate(block_list(level)):
-        if col < 0:
-            turned = [left6(get(p, k + 1).T) for p in (0, 1)]
-        parts = [get(p, level + 2 + i) - dot16(turned[p], found[p][col + 1]) for p in (0, 1)]
-        middle[block(i), :] = parts[0] + parts[1]
+        cols = slice(i * R, (i + 1) * R)
+        weights[i] = jnp.where(which[0] == 0, found[0][:, cols], found[1][:, cols])
+    found = [right6(value) for value in found]
+    at = 0
+    for k in range(level - 1, -1, -1):
+        change = [dot16(left6(get(p, k + 1).T), found[p][:, : (k + 2) * R]) for p in (0, 1)]
+        for i in range(k + 2):
+            cols = slice(i * R, (i + 1) * R)
+            parts = [get(p, level + 2 + at) - change[p][:, cols] for p in (0, 1)]
+            middle[block(at), :] = parts[0] + parts[1]
+            at += 1
     eliminate(level - 1, middle, above, left, give, core, power, result)
 
 
@@ -449,22 +456,19 @@
 
 
 def chain_kernel(*refs):
-    *weights, plain, slope = refs
+    *weights, out = refs
     for k, w in enumerate(weights):
-        value, factor = w[0], -w[1]
+        value = jnp.concatenate([w[0], -w[1]], axis=1)
         for j in range(k):
-            left = left6(w[j + 2])
-            value = value - dot16(left, right6(plain[j]))
-            factor = factor - dot16(left, right6(slope[j]))
-        plain[k] = value
-        slope[k] = factor
+            value = value - dot(w[j + 2], out[j])
+        out[k] = value
 
 
 def chain(weights):
     count = len(weights)
     return pl.pallas_call(
         chain_kernel,
-        out_shape=[jax.ShapeDtypeStruct((count, R, R), F32)] * 2,
+        out_shape=jax.ShapeDtypeStruct((count, R, 2 * R), F32),
         compiler_params=pltpu.CompilerParams(vmem_limit_bytes=8 * MIB),
         cost_estimate=pl.CostEstimate(
             flops=40 * 2 * R**3, bytes_accessed=20 * 4 * R * R, transcendentals=0
@@ -474,7 +478,7 @@
 
 
 def apply_kernel(levels, scales, core, before, mine, other, *refs):
-    weights, (plain, slope), refs = refs[: levels - 1], refs[levels - 1 : levels + 1], refs[levels + 1 :]
+    weights, chained, refs = refs[: levels - 1], refs[levels - 1], refs[levels:]
     given, refs = refs[: 2 * levels + 1], refs[2 * levels + 1 :]
     solved, node_weights, highs, lows, base, out, coefs, total, power, result, *refs = refs
     in_sem, out_sem = refs
@@ -507,7 +511,7 @@
     root = right6(root)
     for k in range(1, levels):
         node_weights[k] = weights[k - 1][0]
-        found.append(plain[k - 1] + dot16(left6(slope[k - 1]), root))
+        found.append(chained[k - 1, :, :R] + dot16(left6(chained[k - 1, :, R:]), root))
     for k in range(levels):
         h, l = split(found[k] * scales[k])
         coefs[block(k), 0:R] = h
@@ -533,7 +537,7 @@
     return pl.pallas_call(
         functools.partial(apply_kernel, levels, scales),
         in_specs=[pl.BlockSpec(memory_space=pltpu.SMEM)]
-        + [vmem] * (len(incoming) + len(weights) + 2)
+        + [vmem] * (len(incoming) + len(weights) + 1)
         + [hbm] * (len(placed) + 1),
         out_specs=[hbm, vmem],
         out_shape=[
@@ -554,7 +558,7 @@
         ],
         compiler_params=pltpu.CompilerParams(vmem_limit_bytes=52 * MIB),
         name="apply",
-    )(core, *incoming, *weights, *chained, *placed, base)
+    )(core, *incoming, *weights, chained, *placed, base)
 
 
 def on_device(tree_order, targets, noise_var, node_bases):

time: 108 us -> 106 us (0.981); the launches traced: 107 us -> 106 us
  no operation moved by 1% of the time
where the time goes in v5:
time: 106 us
  Pallas kernels  58.4 us (55%)
  starting transfers between devices  28.4 us (27%)
  waiting for transfers between devices  14.4 us (14%)
  local copies, waits for them, and re-layouts  3.43 us (3%)
    pallas_call x3, Pallas kernels, place(): pl.pallas_call(functools.partial(place_kernel, levels, with_base), in_spe...  23.4 us
    ppermute x6, starting transfers between devices, swap(): return lax.ppermute(value, axes, [(i, i ^ flip) for i in range(count)])  15.6 us
    pallas_call x1, Pallas kernels, grams(): pl.pallas_call(functools.partial(gram_kernel, levels, scales), in_specs=[...  11.6 us
    ppermute x6, waiting for transfers between devices, swap(): return lax.ppermute(value, axes, [(i, i ^ flip) for i in range(count)])  9.94 us
    pallas_call x1, Pallas kernels, solve_pair(): pl.pallas_call(functools.partial(pair_kernel, level), in_specs=[smem, sme...  9.67 us
    pallas_call x1, Pallas kernels, apply(): pl.pallas_call(functools.partial(apply_kernel, levels, scales), in_specs=...  8.58 us
    all_to_all x1, starting transfers between devices, on_device(): lax.all_to_all(a, ('pair', 'y', 'x'), 0, 0)  7.8 us
    all_to_all x1, starting transfers between devices, on_device(): lax.all_to_all(a, ('y', 'x'), 0, 0)  5 us
  transfers between devices with their start and end apart: 8, of which 8 were waited for; matrix products, arithmetic and copies ran while one was open for 0% of the time, Pallas kernels for 22%

profile of v5, /device:TPU:1, one launch (start us, length us, event | category | flops | bytes accessed | tf_op | source)
XLA Modules:
  0.0 106.4 jit_solution(1477690731726592285)
XLA Ops:
  2.1 11.6 %grams.1 = (f32[896,128]{1,0:T(8,128)S(1)}, f32[896,128]{1,0:T(8,128)S(1)}) custom-call(s32[1]{0:T(128)} %bitcast.core, s32[4096]{0:T(1024)S(1)} %bitcast.8, f32[32,128]{1,0:T(8,128)S(1)} %bitcast.12, f32[4096,128]{1,0:T(8,128)} %refs_0_.1, f32[4,4096,128]{2,1,0:T(8,128)} %bases.7), custom_call_target="tpu_custom_call" | custom-call | tf_op jit(solution)/shard_map/grams/pallas_call | solution.py:150
  13.7 3.3 %collective-permute-start = (f32[896,128]{1,0:T(8,128)S(1)}, f32[896,128]{1,0:T(8,128)S(1)}, u32[]{:S(2)}, u32[]{:S(2)}) collective-permute-start(f32[896,128]{1,0:T(8,128)S(1)} %get-tuple-element.38), channel_id=1, source_target_pairs={{0,1},{1,0},{2,3},{3,2},{4,5},{5,4},{6,7},{7,6},{8,9},{9,8},{10,11... | collective-permute-start | bytes 1376264 | tf_op jit(solution)/shard_map/ppermute | solution.py:580
  17.0 1.4 %collective-permute-done = f32[896,128]{1,0:T(8,128)S(1)} collective-permute-done((f32[896,128]{1,0:T(8,128)S(1)}, f32[896,128]{1,0:T(8,128)S(1)}, u32[]{:S(2)}, u32[]{:S(2)}) %collective-permute-start) | collective-permute-done | bytes 458784 | tf_op jit(solution)/shard_map/ppermute | solution.py:580
  18.5 0.8 add.3
  19.3 5.0 %all-to-all-start = ((f32[16,56,128]{2,1,0:T(8,128)}), f32[16,56,128]{2,1,0:T(8,128)S(1)}, u32[]{:S(2)}, u32[]{:S(2)}) async-start(f32[16,56,128]{2,1,0:T(8,128)} %bitcast.4), calls=%async_computation | async-start | bytes 917504 | tf_op jit(solution)/shard_map/all_to_all | solution.py:595
  24.3 8.4 %place.3 = (bf16[4096,128]{1,0:T(8,128)(2,1)S(1)}, bf16[4096,128]{1,0:T(8,128)(2,1)}, bf16[4096,128]{1,0:T(8,128)(2,1)}, bf16[4096,128]{1,0:T(8,128)(2,1)}) custom-call(s32[4096]{0:T(1024)S(1)} %bitcast.9, f32[32,128]{1,0:T(8,128)S(1)} %bitcast.13, f32[4,4096,128]{2,1,0:T(8,128)} %bases.7), custom_call_target="tpu_custom_call" | custom-call | flops 20971520 | bytes 11534336 | tf_op jit(solution)/shard_map/place/pallas_call | solution.py:431
  32.7 1.0 copy-done
  34.2 1.0 sum_parts.1
  35.2 7.8 %all-to-all-start.1 = ((f32[32,56,128]{2,1,0:T(8,128)}), f32[32,56,128]{2,1,0:T(8,128)S(1)}, u32[]{:S(2)}, u32[]{:S(2)}) async-start(f32[32,56,128]{2,1,0:T(8,128)} %sum_parts.1), calls=%async_computation.1 | async-start | bytes 1835008 | tf_op jit(solution)/shard_map/all_to_all | solution.py:600
  43.0 8.4 %place.4 = (bf16[4096,128]{1,0:T(8,128)(2,1)S(1)}, bf16[4096,128]{1,0:T(8,128)(2,1)}, bf16[4096,128]{1,0:T(8,128)(2,1)}, bf16[4096,128]{1,0:T(8,128)(2,1)}) custom-call(s32[4096]{0:T(1024)S(1)} %bitcast.10, f32[32,128]{1,0:T(8,128)S(1)} %bitcast.14, f32[4,4096,128]{2,1,0:T(8,128)} %bases.7), custom_call_target="tpu_custom_call" | custom-call | flops 20971520 | bytes 11534336 | tf_op jit(solution)/shard_map/place/pallas_call | solution.py:431
  51.5 1.0 copy-done.1
  52.5 4.0 %all-to-all-done.1 = f32[32,56,128]{2,1,0:T(8,128)S(1)} async-done(((f32[32,56,128]{2,1,0:T(8,128)}), f32[32,56,128]{2,1,0:T(8,128)S(1)}, u32[]{:S(2)}, u32[]{:S(2)}) %all-to-all-start.1) | async-done | bytes 917536 | tf_op jit(solution)/shard_map/all_to_all | solution.py:600
  56.4 3.1 %collective-permute-start.1 = (f32[2,896,128]{2,1,0:T(8,128)S(1)}, f32[2,896,128]{2,1,0:T(8,128)S(1)}, u32[]{:S(2)}, u32[]{:S(2)}) collective-permute-start(f32[2,896,128]{2,1,0:T(8,128)S(1)} %bitcast.6), channel_id=1, source_target_pairs={{0,1},{1,0},{2,3},{3,2},{4,5},{5,4},{6,7},{7,6},{8,9},{9,8},{10,11... | collective-permute-start | bytes 2752520 | tf_op jit(solution)/shard_map/ppermute | solution.py:580
  59.5 2.1 %collective-permute-done.1.other = f32[2,896,128]{2,1,0:T(8,128)S(1)} collective-permute-done((f32[2,896,128]{2,1,0:T(8,128)S(1)}, f32[2,896,128]{2,1,0:T(8,128)S(1)}, u32[]{:S(2)}, u32[]{:S(2)}) %collective-permute-start.1) | collective-permute-done | bytes 917536 | tf_op jit(solution)/shard_map/ppermute | solution.py:580
  61.6 9.7 %pair.1 = (f32[4,128,128]{2,1,0:T(8,128)S(1)}, f32[3,128,128]{2,1,0:T(8,128)S(1)}, f32[640,128]{1,0:T(8,128)S(1)}, f32[320,128]{1,0:T(8,128)S(1)}) custom-call(s32[1]{0:T(128)} %bitcast.core, s32[1]{0:T(128)} %bitcast.1.which, f32[2,896,128]{2,1,0:T(8,128)S(1)} %bitcast.7, f32[2,896,128]{2,1,0:T(8,128)S(1)} %collective-permute-done.1.other), custom_call_target="tpu_custom_call" | custom-call | tf_op jit(solution)/shard_map/pair/pallas_call | solution.py:310
  71.3 4.3 %collective-permute-start.2 = (f32[320,128]{1,0:T(8,128)S(1)}, f32[320,128]{1,0:T(8,128)S(1)}, u32[]{:S(2)}, u32[]{:S(2)}) collective-permute-start(f32[320,128]{1,0:T(8,128)S(1)} %get-tuple-element.55), channel_id=1, source_target_pairs={{0,4},{1,5},{2,6},{3,7},{4,0},{5,1},{6,2},{7,3},{8,12},{9,13},{10,... | collective-permute-start | bytes 491528 | tf_op jit(solution)/shard_map/ppermute | solution.py:580
  75.6 6.5 %place.5.refs_12_ = f32[4096,128]{1,0:T(8,128)} custom-call(s32[4096]{0:T(1024)S(1)} %bitcast.11, f32[32,128]{1,0:T(8,128)S(1)} %bitcast.15, f32[4,4096,128]{2,1,0:T(8,128)} %bases.7, f32[4096,128]{1,0:T(8,128)} %refs_0_.1), custom_call_target="tpu_custom_call" | custom-call | flops 20971520 | bytes 11534336 | tf_op jit(solution)/shard_map/place/pallas_call | solution.py:431
  82.2 1.2 %collective-permute-done.2.mine = f32[320,128]{1,0:T(8,128)S(1)} collective-permute-done((f32[320,128]{1,0:T(8,128)S(1)}, f32[320,128]{1,0:T(8,128)S(1)}, u32[]{:S(2)}, u32[]{:S(2)}) %collective-permute-start.2) | collective-permute-done | bytes 163872 | tf_op jit(solution)/shard_map/ppermute | solution.py:580
  83.4 0.9 collective-permute-start.3
  84.3 1.0 collective-permute-done.3.other
  85.3 3.7 %level.1 = (f32[2,128,128]{2,1,0:T(8,128)S(1)}, f32[256,128]{1,0:T(8,128)S(1)}, f32[128,128]{1,0:T(8,128)S(1)}) custom-call(s32[1]{0:T(128)} %bitcast.core, f32[640,128]{1,0:T(8,128)S(1)} %get-tuple-element.53.before, f32[320,128]{1,0:T(8,128)S(1)} %collective-permute-done.2.mine, f32[320,128]{1,0:T(8,128)S(1)} %collective-permute-done.3.other), custom_call_target="tpu_custom_call" | custom-call | tf_op jit(solution)/shard_map/level/pallas_call | solution.py:335
  89.1 3.2 %collective-permute-start.4 = (f32[128,128]{1,0:T(8,128)S(1)}, f32[128,128]{1,0:T(8,128)S(1)}, u32[]{:S(2)}, u32[]{:S(2)}) collective-permute-start(f32[128,128]{1,0:T(8,128)S(1)} %get-tuple-element.59), channel_id=1, source_target_pairs={{0,14},{1,15},{2,12},{3,13},{4,10},{5,11},{6,8},{7,9},{8,6},{9,7},... | collective-permute-start | bytes 196616 | tf_op jit(solution)/shard_map/ppermute | solution.py:580
  92.3 3.7 %collective-permute-done.4.mine = f32[128,128]{1,0:T(8,128)S(1)} collective-permute-done((f32[128,128]{1,0:T(8,128)S(1)}, f32[128,128]{1,0:T(8,128)S(1)}, u32[]{:S(2)}, u32[]{:S(2)}) %collective-permute-start.4) | collective-permute-done | bytes 65568 | tf_op jit(solution)/shard_map/ppermute | solution.py:580
  97.6 8.6 %apply.1 = (f32[4096,128]{1,0:T(8,128)}, f32[4,128,128]{2,1,0:T(8,128)}) custom-call(s32[1]{0:T(128)} %bitcast.core, f32[256,128]{1,0:T(8,128)S(1)} %get-tuple-element.58.before, f32[128,128]{1,0:T(8,128)S(1)} %collective-permute-done.4.mine, f32[128,128]{1,0:T(8,128)S(1)} %collective-permute-done.5.other, f32[2,128,128]{2,1,0:T(8,128)S(1)} %get-tuple-element.60.refs_0_, ...), custom_call_target="tpu_custom_call" | custom-call | tf_op jit(solution)/shard_map/apply/pallas_call | solution.py:537
  (14 shorter events, 3.6 us)
Async XLA Ops:
  0.6 0.7 copy-start.2
  1.4 0.7 copy-start.4
  13.7 10.6 %copy-start.3 = (s32[1,4096]{1,0:T(1,128)S(1)}, s32[1,4096]{1,0:T(1,128)}, u32[]{:S(2)}) copy-start(s32[1,4096]{1,0:T(1,128)} %param.4) | copy-start | bytes 49156
  13.7 10.6 %copy-start.5 = (f32[4096]{0:T(1024)S(1)}, f32[4096]{0:T(1024)}, u32[]{:S(2)}) copy-start(f32[4096]{0:T(1024)} %param.6) | copy-start | bytes 49156
  13.7 4.8 %collective-permute-start = (f32[896,128]{1,0:T(8,128)S(1)}, f32[896,128]{1,0:T(8,128)S(1)}, u32[]{:S(2)}, u32[]{:S(2)}) collective-permute-start(f32[896,128]{1,0:T(8,128)S(1)} %get-tuple-element.38), channel_id=1, source_target_pairs={{0,1},{1,0},{2,3},{3,2},{4,5},{5,4},{6,7},{7,6},{8,9},{9,8},{10,11... | collective-permute-start | bytes 1376264 | tf_op jit(solution)/shard_map/ppermute | solution.py:580
  19.3 14.9 %all-to-all-start = ((f32[16,56,128]{2,1,0:T(8,128)}), f32[16,56,128]{2,1,0:T(8,128)S(1)}, u32[]{:S(2)}, u32[]{:S(2)}) async-start(f32[16,56,128]{2,1,0:T(8,128)} %bitcast.4), calls=%async_computation | async-start | bytes 917504 | tf_op jit(solution)/shard_map/all_to_all | solution.py:595
  32.7 1.0 copy-start
  35.2 21.2 %all-to-all-start.1 = ((f32[32,56,128]{2,1,0:T(8,128)}), f32[32,56,128]{2,1,0:T(8,128)S(1)}, u32[]{:S(2)}, u32[]{:S(2)}) async-start(f32[32,56,128]{2,1,0:T(8,128)} %sum_parts.1), calls=%async_computation.1 | async-start | bytes 1835008 | tf_op jit(solution)/shard_map/all_to_all | solution.py:600
  51.5 1.0 copy-start.1
  56.4 5.2 %collective-permute-start.1 = (f32[2,896,128]{2,1,0:T(8,128)S(1)}, f32[2,896,128]{2,1,0:T(8,128)S(1)}, u32[]{:S(2)}, u32[]{:S(2)}) collective-permute-start(f32[2,896,128]{2,1,0:T(8,128)S(1)} %bitcast.6), channel_id=1, source_target_pairs={{0,1},{1,0},{2,3},{3,2},{4,5},{5,4},{6,7},{7,6},{8,9},{9,8},{10,11... | collective-permute-start | bytes 2752520 | tf_op jit(solution)/shard_map/ppermute | solution.py:580
  71.3 12.1 %collective-permute-start.2 = (f32[320,128]{1,0:T(8,128)S(1)}, f32[320,128]{1,0:T(8,128)S(1)}, u32[]{:S(2)}, u32[]{:S(2)}) collective-permute-start(f32[320,128]{1,0:T(8,128)S(1)} %get-tuple-element.55), channel_id=1, source_target_pairs={{0,4},{1,5},{2,6},{3,7},{4,0},{5,1},{6,2},{7,3},{8,12},{9,13},{10,... | collective-permute-start | bytes 491528 | tf_op jit(solution)/shard_map/ppermute | solution.py:580
  83.4 1.9 %collective-permute-start.3 = (f32[320,128]{1,0:T(8,128)S(1)}, f32[320,128]{1,0:T(8,128)S(1)}, u32[]{:S(2)}, u32[]{:S(2)}) collective-permute-start(f32[320,128]{1,0:T(8,128)S(1)} %collective-permute-done.2.mine), channel_id=1, source_target_pairs={{0,1},{1,0},{2,3},{3,2},{4,5},{5,4},{6,7},{7,6},{8,9},{9,8},{10,11... | collective-permute-start | bytes 491528 | tf_op jit(solution)/shard_map/ppermute | solution.py:580
  89.1 6.9 %collective-permute-start.4 = (f32[128,128]{1,0:T(8,128)S(1)}, f32[128,128]{1,0:T(8,128)S(1)}, u32[]{:S(2)}, u32[]{:S(2)}) collective-permute-start(f32[128,128]{1,0:T(8,128)S(1)} %get-tuple-element.59), channel_id=1, source_target_pairs={{0,14},{1,15},{2,12},{3,13},{4,10},{5,11},{6,8},{7,9},{8,6},{9,7},... | collective-permute-start | bytes 196616 | tf_op jit(solution)/shard_map/ppermute | solution.py:580
  96.0 1.6 %collective-permute-start.5 = (f32[128,128]{1,0:T(8,128)S(1)}, f32[128,128]{1,0:T(8,128)S(1)}, u32[]{:S(2)}, u32[]{:S(2)}) collective-permute-start(f32[128,128]{1,0:T(8,128)S(1)} %collective-permute-done.4.mine), channel_id=1, source_target_pairs={{0,1},{1,0},{2,3},{3,2},{4,5},{5,4},{6,7},{7,6},{8,9},{9,8},{10,11... | collective-permute-start | bytes 196616 | tf_op jit(solution)/shard_map/ppermute | solution.py:580

commit v6 on v5

--- a/solution.py
+++ b/solution.py
@@ -199,17 +199,19 @@
         low = jnp.maximum(jnp.min(diagonal - radius), 1.0)
         factor = 2.0 / (low + top)
         bound = jnp.maximum(bound, (top - low) / (low + top))
-        power[i] = eye - factor * c
-        result[i] = factor * (eye + power[i])
+        e = eye - factor * c
+        result[i] = factor * (eye + e)
+        power[i] = dot(e, e)
 
     def cond(bound):
         return bound > 1e-4
 
     def body(bound):
         for i in range(len(several)):
-            e = dot(power[i], power[i])
-            power[i] = e
-            result[i] += dot(result[i], e)
+            e, x = power[i], result[i]
+            both = dot(jnp.concatenate([e, x], axis=0), e)
+            power[i] = both[:n, :]
+            result[i] = x + both[n:, :]
         return bound * bound
 
     lax.while_loop(cond, body, bound * bound)

time: 106 us -> 103 us (0.972)
  Pallas kernels: 58.4 us -> 55.5 us
    pallas_call x1, Pallas kernels: 9.67 us -> 7.86 us  [solve_pair(): pl.pallas_call(functools.partial(pair_kernel, level), in_specs=[smem, sme...]
  transfers between devices with their start and end apart: 8 -> 8, of which waited for: 8 -> 8; matrix products, arithmetic and copies ran while one was open for 0% -> 0% of each run, Pallas kernels for 22% -> 23%
where the time goes in v6:
time: 103 us
  Pallas kernels  55.5 us (54%)
  starting transfers between devices  28.2 us (27%)
  waiting for transfers between devices  13.8 us (13%)
  local copies, waits for them, and re-layouts  3.43 us (3%)
    pallas_call x3, Pallas kernels, place(): pl.pallas_call(functools.partial(place_kernel, levels, with_base), in_spe...  23.4 us
    ppermute x6, starting transfers between devices, swap(): return lax.ppermute(value, axes, [(i, i ^ flip) for i in range(count)])  15.4 us
    pallas_call x1, Pallas kernels, grams(): pl.pallas_call(functools.partial(gram_kernel, levels, scales), in_specs=[...  11.6 us
    ppermute x6, waiting for transfers between devices, swap(): return lax.ppermute(value, axes, [(i, i ^ flip) for i in range(count)])  9.38 us
    pallas_call x1, Pallas kernels, apply(): pl.pallas_call(functools.partial(apply_kernel, levels, scales), in_specs=...  8.02 us
    pallas_call x1, Pallas kernels, solve_pair(): pl.pallas_call(functools.partial(pair_kernel, level), in_specs=[smem, sme...  7.86 us
    all_to_all x1, starting transfers between devices, on_device(): lax.all_to_all(a, ('pair', 'y', 'x'), 0, 0)  7.79 us
    all_to_all x1, starting transfers between devices, on_device(): lax.all_to_all(a, ('y', 'x'), 0, 0)  5.01 us
  transfers between devices with their start and end apart: 8, of which 8 were waited for; matrix products, arithmetic and copies ran while one was open for 0% of the time, Pallas kernels for 23%

profile of v6, /device:TPU:1, one launch (start us, length us, event | category | flops | bytes accessed | tf_op | source)
XLA Modules:
  0.0 102.8 jit_solution(7583834313656707859)
XLA Ops:
  2.1 11.6 %grams.1 = (f32[896,128]{1,0:T(8,128)S(1)}, f32[896,128]{1,0:T(8,128)S(1)}) custom-call(s32[1]{0:T(128)} %bitcast.core, s32[4096]{0:T(1024)S(1)} %bitcast.8, f32[32,128]{1,0:T(8,128)S(1)} %bitcast.12, f32[4096,128]{1,0:T(8,128)} %refs_0_.1, f32[4,4096,128]{2,1,0:T(8,128)} %bases.7), custom_call_target="tpu_custom_call" | custom-call | tf_op jit(solution)/shard_map/grams/pallas_call | solution.py:150
  13.7 3.3 %collective-permute-start = (f32[896,128]{1,0:T(8,128)S(1)}, f32[896,128]{1,0:T(8,128)S(1)}, u32[]{:S(2)}, u32[]{:S(2)}) collective-permute-start(f32[896,128]{1,0:T(8,128)S(1)} %get-tuple-element.38), channel_id=1, source_target_pairs={{0,1},{1,0},{2,3},{3,2},{4,5},{5,4},{6,7},{7,6},{8,9},{9,8},{10,11... | collective-permute-start | bytes 1376264 | tf_op jit(solution)/shard_map/ppermute | solution.py:582
  17.0 1.4 %collective-permute-done = f32[896,128]{1,0:T(8,128)S(1)} collective-permute-done((f32[896,128]{1,0:T(8,128)S(1)}, f32[896,128]{1,0:T(8,128)S(1)}, u32[]{:S(2)}, u32[]{:S(2)}) %collective-permute-start) | collective-permute-done | bytes 458784 | tf_op jit(solution)/shard_map/ppermute | solution.py:582
  18.5 0.8 add.3
  19.3 5.0 %all-to-all-start = ((f32[16,56,128]{2,1,0:T(8,128)}), f32[16,56,128]{2,1,0:T(8,128)S(1)}, u32[]{:S(2)}, u32[]{:S(2)}) async-start(f32[16,56,128]{2,1,0:T(8,128)} %bitcast.4), calls=%async_computation | async-start | bytes 917504 | tf_op jit(solution)/shard_map/all_to_all | solution.py:597
  24.3 8.4 %place.3 = (bf16[4096,128]{1,0:T(8,128)(2,1)S(1)}, bf16[4096,128]{1,0:T(8,128)(2,1)}, bf16[4096,128]{1,0:T(8,128)(2,1)}, bf16[4096,128]{1,0:T(8,128)(2,1)}) custom-call(s32[4096]{0:T(1024)S(1)} %bitcast.9, f32[32,128]{1,0:T(8,128)S(1)} %bitcast.13, f32[4,4096,128]{2,1,0:T(8,128)} %bases.7), custom_call_target="tpu_custom_call" | custom-call | flops 20971520 | bytes 11534336 | tf_op jit(solution)/shard_map/place/pallas_call | solution.py:433
  32.7 1.0 copy-done
  34.2 1.0 sum_parts.1
  35.2 7.8 %all-to-all-start.1 = ((f32[32,56,128]{2,1,0:T(8,128)}), f32[32,56,128]{2,1,0:T(8,128)S(1)}, u32[]{:S(2)}, u32[]{:S(2)}) async-start(f32[32,56,128]{2,1,0:T(8,128)} %sum_parts.1), calls=%async_computation.1 | async-start | bytes 1835008 | tf_op jit(solution)/shard_map/all_to_all | solution.py:602
  43.0 8.4 %place.4 = (bf16[4096,128]{1,0:T(8,128)(2,1)S(1)}, bf16[4096,128]{1,0:T(8,128)(2,1)}, bf16[4096,128]{1,0:T(8,128)(2,1)}, bf16[4096,128]{1,0:T(8,128)(2,1)}) custom-call(s32[4096]{0:T(1024)S(1)} %bitcast.10, f32[32,128]{1,0:T(8,128)S(1)} %bitcast.14, f32[4,4096,128]{2,1,0:T(8,128)} %bases.7), custom_call_target="tpu_custom_call" | custom-call | flops 20971520 | bytes 11534336 | tf_op jit(solution)/shard_map/place/pallas_call | solution.py:433
  51.5 1.0 copy-done.1
  52.5 4.0 %all-to-all-done.1 = f32[32,56,128]{2,1,0:T(8,128)S(1)} async-done(((f32[32,56,128]{2,1,0:T(8,128)}), f32[32,56,128]{2,1,0:T(8,128)S(1)}, u32[]{:S(2)}, u32[]{:S(2)}) %all-to-all-start.1) | async-done | bytes 917536 | tf_op jit(solution)/shard_map/all_to_all | solution.py:602
  56.4 3.1 %collective-permute-start.1 = (f32[2,896,128]{2,1,0:T(8,128)S(1)}, f32[2,896,128]{2,1,0:T(8,128)S(1)}, u32[]{:S(2)}, u32[]{:S(2)}) collective-permute-start(f32[2,896,128]{2,1,0:T(8,128)S(1)} %bitcast.6), channel_id=1, source_target_pairs={{0,1},{1,0},{2,3},{3,2},{4,5},{5,4},{6,7},{7,6},{8,9},{9,8},{10,11... | collective-permute-start | bytes 2752520 | tf_op jit(solution)/shard_map/ppermute | solution.py:582
  59.5 2.1 %collective-permute-done.1.other = f32[2,896,128]{2,1,0:T(8,128)S(1)} collective-permute-done((f32[2,896,128]{2,1,0:T(8,128)S(1)}, f32[2,896,128]{2,1,0:T(8,128)S(1)}, u32[]{:S(2)}, u32[]{:S(2)}) %collective-permute-start.1) | collective-permute-done | bytes 917536 | tf_op jit(solution)/shard_map/ppermute | solution.py:582
  61.6 7.9 %pair.1 = (f32[4,128,128]{2,1,0:T(8,128)S(1)}, f32[3,128,128]{2,1,0:T(8,128)S(1)}, f32[640,128]{1,0:T(8,128)S(1)}, f32[320,128]{1,0:T(8,128)S(1)}) custom-call(s32[1]{0:T(128)} %bitcast.core, s32[1]{0:T(128)} %bitcast.1.which, f32[2,896,128]{2,1,0:T(8,128)S(1)} %bitcast.7, f32[2,896,128]{2,1,0:T(8,128)S(1)} %collective-permute-done.1.other), custom_call_target="tpu_custom_call" | custom-call | tf_op jit(solution)/shard_map/pair/pallas_call | solution.py:312
  69.5 3.3 %collective-permute-start.2 = (f32[320,128]{1,0:T(8,128)S(1)}, f32[320,128]{1,0:T(8,128)S(1)}, u32[]{:S(2)}, u32[]{:S(2)}) collective-permute-start(f32[320,128]{1,0:T(8,128)S(1)} %get-tuple-element.55), channel_id=1, source_target_pairs={{0,4},{1,5},{2,6},{3,7},{4,0},{5,1},{6,2},{7,3},{8,12},{9,13},{10,... | collective-permute-start | bytes 491528 | tf_op jit(solution)/shard_map/ppermute | solution.py:582
  72.7 6.5 %place.5.refs_12_ = f32[4096,128]{1,0:T(8,128)} custom-call(s32[4096]{0:T(1024)S(1)} %bitcast.11, f32[32,128]{1,0:T(8,128)S(1)} %bitcast.15, f32[4,4096,128]{2,1,0:T(8,128)} %bases.7, f32[4096,128]{1,0:T(8,128)} %refs_0_.1), custom_call_target="tpu_custom_call" | custom-call | flops 20971520 | bytes 11534336 | tf_op jit(solution)/shard_map/place/pallas_call | solution.py:433
  79.3 1.2 %collective-permute-done.2.mine = f32[320,128]{1,0:T(8,128)S(1)} collective-permute-done((f32[320,128]{1,0:T(8,128)S(1)}, f32[320,128]{1,0:T(8,128)S(1)}, u32[]{:S(2)}, u32[]{:S(2)}) %collective-permute-start.2) | collective-permute-done | bytes 163872 | tf_op jit(solution)/shard_map/ppermute | solution.py:582
  80.5 0.9 collective-permute-start.3
  81.4 1.0 %collective-permute-done.3.other = f32[320,128]{1,0:T(8,128)S(1)} collective-permute-done((f32[320,128]{1,0:T(8,128)S(1)}, f32[320,128]{1,0:T(8,128)S(1)}, u32[]{:S(2)}, u32[]{:S(2)}) %collective-permute-start.3) | collective-permute-done | bytes 163872 | tf_op jit(solution)/shard_map/ppermute | solution.py:582
  82.4 3.2 %level.1 = (f32[2,128,128]{2,1,0:T(8,128)S(1)}, f32[256,128]{1,0:T(8,128)S(1)}, f32[128,128]{1,0:T(8,128)S(1)}) custom-call(s32[1]{0:T(128)} %bitcast.core, f32[640,128]{1,0:T(8,128)S(1)} %get-tuple-element.53.before, f32[320,128]{1,0:T(8,128)S(1)} %collective-permute-done.2.mine, f32[320,128]{1,0:T(8,128)S(1)} %collective-permute-done.3.other), custom_call_target="tpu_custom_call" | custom-call | tf_op jit(solution)/shard_map/level/pallas_call | solution.py:337
  85.6 4.3 %collective-permute-start.4 = (f32[128,128]{1,0:T(8,128)S(1)}, f32[128,128]{1,0:T(8,128)S(1)}, u32[]{:S(2)}, u32[]{:S(2)}) collective-permute-start(f32[128,128]{1,0:T(8,128)S(1)} %get-tuple-element.59), channel_id=1, source_target_pairs={{0,14},{1,15},{2,12},{3,13},{4,10},{5,11},{6,8},{7,9},{8,6},{9,7},... | collective-permute-start | bytes 196616 | tf_op jit(solution)/shard_map/ppermute | solution.py:582
  89.9 3.2 %collective-permute-done.4.mine = f32[128,128]{1,0:T(8,128)S(1)} collective-permute-done((f32[128,128]{1,0:T(8,128)S(1)}, f32[128,128]{1,0:T(8,128)S(1)}, u32[]{:S(2)}, u32[]{:S(2)}) %collective-permute-start.4) | collective-permute-done | bytes 65568 | tf_op jit(solution)/shard_map/ppermute | solution.py:582
  94.6 8.0 %apply.1 = (f32[4096,128]{1,0:T(8,128)}, f32[4,128,128]{2,1,0:T(8,128)}) custom-call(s32[1]{0:T(128)} %bitcast.core, f32[256,128]{1,0:T(8,128)S(1)} %get-tuple-element.58.before, f32[128,128]{1,0:T(8,128)S(1)} %collective-permute-done.4.mine, f32[128,128]{1,0:T(8,128)S(1)} %collective-permute-done.5.other, f32[2,128,128]{2,1,0:T(8,128)S(1)} %get-tuple-element.60.refs_0_, ...), custom_call_target="tpu_custom_call" | custom-call | tf_op jit(solution)/shard_map/apply/pallas_call | solution.py:539
  (14 shorter events, 3.4 us)
Async XLA Ops:
  0.6 0.7 copy-start.2
  1.4 0.7 copy-start.4
  13.7 10.6 %copy-start.3 = (s32[1,4096]{1,0:T(1,128)S(1)}, s32[1,4096]{1,0:T(1,128)}, u32[]{:S(2)}) copy-start(s32[1,4096]{1,0:T(1,128)} %param.4) | copy-start | bytes 49156
  13.7 10.6 %copy-start.5 = (f32[4096]{0:T(1024)S(1)}, f32[4096]{0:T(1024)}, u32[]{:S(2)}) copy-start(f32[4096]{0:T(1024)} %param.6) | copy-start | bytes 49156
  13.7 4.7 %collective-permute-start = (f32[896,128]{1,0:T(8,128)S(1)}, f32[896,128]{1,0:T(8,128)S(1)}, u32[]{:S(2)}, u32[]{:S(2)}) collective-permute-start(f32[896,128]{1,0:T(8,128)S(1)} %get-tuple-element.38), channel_id=1, source_target_pairs={{0,1},{1,0},{2,3},{3,2},{4,5},{5,4},{6,7},{7,6},{8,9},{9,8},{10,11... | collective-permute-start | bytes 1376264 | tf_op jit(solution)/shard_map/ppermute | solution.py:582
  19.3 14.9 %all-to-all-start = ((f32[16,56,128]{2,1,0:T(8,128)}), f32[16,56,128]{2,1,0:T(8,128)S(1)}, u32[]{:S(2)}, u32[]{:S(2)}) async-start(f32[16,56,128]{2,1,0:T(8,128)} %bitcast.4), calls=%async_computation | async-start | bytes 917504 | tf_op jit(solution)/shard_map/all_to_all | solution.py:597
  32.7 1.0 copy-start
  35.2 21.2 %all-to-all-start.1 = ((f32[32,56,128]{2,1,0:T(8,128)}), f32[32,56,128]{2,1,0:T(8,128)S(1)}, u32[]{:S(2)}, u32[]{:S(2)}) async-start(f32[32,56,128]{2,1,0:T(8,128)} %sum_parts.1), calls=%async_computation.1 | async-start | bytes 1835008 | tf_op jit(solution)/shard_map/all_to_all | solution.py:602
  51.5 1.0 copy-start.1
  56.4 5.2 %collective-permute-start.1 = (f32[2,896,128]{2,1,0:T(8,128)S(1)}, f32[2,896,128]{2,1,0:T(8,128)S(1)}, u32[]{:S(2)}, u32[]{:S(2)}) collective-permute-start(f32[2,896,128]{2,1,0:T(8,128)S(1)} %bitcast.6), channel_id=1, source_target_pairs={{0,1},{1,0},{2,3},{3,2},{4,5},{5,4},{6,7},{7,6},{8,9},{9,8},{10,11... | collective-permute-start | bytes 2752520 | tf_op jit(solution)/shard_map/ppermute | solution.py:582
  69.5 11.0 %collective-permute-start.2 = (f32[320,128]{1,0:T(8,128)S(1)}, f32[320,128]{1,0:T(8,128)S(1)}, u32[]{:S(2)}, u32[]{:S(2)}) collective-permute-start(f32[320,128]{1,0:T(8,128)S(1)} %get-tuple-element.55), channel_id=1, source_target_pairs={{0,4},{1,5},{2,6},{3,7},{4,0},{5,1},{6,2},{7,3},{8,12},{9,13},{10,... | collective-permute-start | bytes 491528 | tf_op jit(solution)/shard_map/ppermute | solution.py:582
  80.5 1.9 %collective-permute-start.3 = (f32[320,128]{1,0:T(8,128)S(1)}, f32[320,128]{1,0:T(8,128)S(1)}, u32[]{:S(2)}, u32[]{:S(2)}) collective-permute-start(f32[320,128]{1,0:T(8,128)S(1)} %collective-permute-done.2.mine), channel_id=1, source_target_pairs={{0,1},{1,0},{2,3},{3,2},{4,5},{5,4},{6,7},{7,6},{8,9},{9,8},{10,11... | collective-permute-start | bytes 491528 | tf_op jit(solution)/shard_map/ppermute | solution.py:582
  85.6 7.5 %collective-permute-start.4 = (f32[128,128]{1,0:T(8,128)S(1)}, f32[128,128]{1,0:T(8,128)S(1)}, u32[]{:S(2)}, u32[]{:S(2)}) collective-permute-start(f32[128,128]{1,0:T(8,128)S(1)} %get-tuple-element.59), channel_id=1, source_target_pairs={{0,14},{1,15},{2,12},{3,13},{4,10},{5,11},{6,8},{7,9},{8,6},{9,7},... | collective-permute-start | bytes 196616 | tf_op jit(solution)/shard_map/ppermute | solution.py:582
  93.1 1.5 %collective-permute-start.5 = (f32[128,128]{1,0:T(8,128)S(1)}, f32[128,128]{1,0:T(8,128)S(1)}, u32[]{:S(2)}, u32[]{:S(2)}) collective-permute-start(f32[128,128]{1,0:T(8,128)S(1)} %collective-permute-done.4.mine), channel_id=1, source_target_pairs={{0,1},{1,0},{2,3},{3,2},{4,5},{5,4},{6,7},{7,6},{8,9},{9,8},{10,11... | collective-permute-start | bytes 196616 | tf_op jit(solution)/shard_map/ppermute | solution.py:582
